TPU v7x, 256 devices: a whole 4x4x8 slice. The times are simulated.
256 devices in a mesh: dp: 16 (over x_hi, y, core), tp: 16 (over z, x_lo).
Axes of the slice: x: 4 (x_hi: 2, x_lo: 2; x = x_hi * 2 + x_lo), y: 4, z: 8, core: 2. Of those that a mesh axis runs over, the one named last changes fastest.
Arguments:
- query: bfloat16 [128, 24576], P('dp', 'tp'), may hold values from -10 to 10
- latent_cache: bfloat16 [128, 2048, 576], P('dp'), may hold values from -8 to 8
- lengths: int32 [128], P('dp'), may hold values from 32 to 2048, as said below
- w_uk: bfloat16 [128, 128, 512], P('tp'), may hold values from -0.5 to 0.5
- value_up_weight: bfloat16 [128, 512, 128], P('tp'), may hold values from -0.25 to 0.25
- w_out: bfloat16 [16384, 7168], P('tp', 'dp'), may hold values from -0.046875 to 0.046875
- residual: bfloat16 [128, 7168], P(None, 'dp'), may hold values from -16 to 16
- mlp_norm_scale: bfloat16 [7168], P('dp'), may hold values from 0.099609375 to 1.8984375
- w_gate: bfloat16 [7168, 18432], P('dp', 'tp'), may hold values from -0.0625 to 0.0625
- w_up: bfloat16 [7168, 18432], P('dp', 'tp'), may hold values from -0.0625 to 0.0625
- w_down: bfloat16 [18432, 7168], P('tp', 'dp'), may hold values from -0.046875 to 0.046875
Outputs:
- mixed: bfloat16 [128, 7168], P('tp', 'dp')
Inputs may be any that keep to these rules, and one draw needn't show every extreme that they name: `lengths`: some request in every draw has all 2048 slots live.
All inputs are finite; a program needn't handle non-finite values.
Results may differ from a plain program's by a relative error of at most 0.025.
Values may be sent and summed in bfloat16 or wider, within the bound.
A program may use at most 128 MiB of HBM per device.

v0:
```python
import jax
import jax.numpy as jnp
from jax import lax
from jax.sharding import PartitionSpec as P

D = 7168
NOPE = 128
ROPE = 64
KVR = 512
VD = 128


def block_scores(q_latent, rotary_query, cache_part, scale):
    latent = cache_part[:, :, :KVR]
    rotary_key = cache_part[:, :, KVR:]
    first = jnp.einsum("rhk,rtk->rht", q_latent, latent, preferred_element_type=jnp.float32)
    second = jnp.einsum(
        "rhe,rte->rht", rotary_query, rotary_key, preferred_element_type=jnp.float32
    )
    return (first + second) * scale


def attend(query, latent_cache, lengths, w_uk, value_up_weight):
    rows = query.shape[0]
    heads = w_uk.shape[0]
    slots = latent_cache.shape[1]
    head_query = query.reshape(rows, heads, NOPE + ROPE)
    q_nope = head_query[:, :, :NOPE]
    rotary_query = head_query[:, :, NOPE:]
    q_latent = jnp.einsum("rhn,hnk->rhk", q_nope, w_uk, preferred_element_type=jnp.float32).astype(
        jnp.bfloat16
    )
    scale = 1.0 / jnp.sqrt(jnp.float32(NOPE + ROPE))
    live = jnp.arange(slots, dtype=jnp.int32)[None, None, :] < lengths[:, None, None]
    scores = block_scores(q_latent, rotary_query, latent_cache, scale)
    scores = jnp.where(live, scores, -jnp.inf)
    probs = jax.nn.softmax(scores, axis=-1).astype(jnp.bfloat16)
    attention_context = jnp.einsum(
        "rht,rtk->rhk", probs, latent_cache[:, :, :KVR], preferred_element_type=jnp.float32
    )
    attention_context = attention_context.astype(jnp.bfloat16)
    value_rows = jnp.einsum(
        "dab,abg->dag", attention_context, value_up_weight, preferred_element_type=jnp.float32
    ).astype(jnp.bfloat16)
    return value_rows.reshape(rows, heads * VD)


def normalize(stream):
    wide = stream.astype(jnp.float32)
    return (wide, jnp.sum(wide * wide, axis=1))


def on_device(
    query,
    latent_cache,
    lengths,
    w_uk,
    value_up_weight,
    w_out,
    residual,
    mlp_norm_scale,
    w_gate,
    w_up,
    w_down,
):
    value_rows = attend(query, latent_cache, lengths, w_uk, value_up_weight)
    partial_out = jnp.dot(
        lax.all_gather(value_rows, "dp", axis=0, tiled=True),
        w_out,
        preferred_element_type=jnp.float32,
    )
    total_rows = partial_out.shape[0]
    block_rows = total_rows // lax.axis_size("tp")
    block_start = lax.axis_index("tp") * block_rows
    gain = mlp_norm_scale.astype(jnp.float32)[None, :]
    attended = lax.psum(partial_out.astype(jnp.bfloat16), "tp").astype(jnp.float32)
    stream = (residual.astype(jnp.float32) + attended).astype(jnp.bfloat16)
    wide, squares = normalize(stream)
    squares = lax.psum(squares, "dp")
    inv_rms = 1.0 / jnp.sqrt(squares / D + 1e-06)
    normed = (wide * inv_rms[:, None] * gain).astype(jnp.bfloat16)
    own_stream = lax.dynamic_slice_in_dim(wide, block_start, block_rows, 0)
    gate = jnp.dot(normed, w_gate, preferred_element_type=jnp.float32)
    up = jnp.dot(normed, w_up, preferred_element_type=jnp.float32)
    gate, up = (
        lax.psum(gate.astype(jnp.bfloat16), "dp").astype(jnp.float32),
        lax.psum(up.astype(jnp.bfloat16), "dp").astype(jnp.float32),
    )
    hidden = (jax.nn.silu(gate) * up).astype(jnp.bfloat16)
    mlp_rows = lax.psum_scatter(
        jnp.dot(hidden, w_down, preferred_element_type=jnp.float32).astype(jnp.bfloat16),
        "tp",
        scatter_dimension=0,
        tiled=True,
    ).astype(jnp.float32)
    return (own_stream + mlp_rows).astype(jnp.bfloat16)


def solution(mesh):
    return jax.shard_map(
        on_device,
        mesh=mesh,
        in_specs=(
            P("dp", "tp"),
            P("dp", None, None),
            P("dp"),
            P("tp", None, None),
            P("tp", None, None),
            P("tp", "dp"),
            P(None, "dp"),
            P("dp"),
            P("dp", "tp"),
            P("dp", "tp"),
            P("tp", "dp"),
        ),
        out_specs=P("tp", "dp"),
        check_vma=False,
    )
```

profile of v0, /device:TPU:8, one launch (start us, length us, event | category | flops | bytes accessed | tf_op | source)
XLA Modules:
  0.0 450.2 jit_solution(11124608592072934312)
XLA Ops:
  6.5 0.9 reshape.31
  7.5 0.7 iota_compare_fusion
  8.2 0.2 fusion.13
  8.5 7.1 %fusion.1 = f32[8,8,2048]{2,1,0:T(8,128)S(1)} fusion(bf16[8,2048,576]{1,2,0:T(8,128)(2,1)} %param.12, bf16[8,8,512]{2,0,1:T(8,128)(2,1)S(1)} %fusion.13), kind=kOutput, calls=%fused_computation.1 | convolution fusion | flops 134217728 | bytes 17367040 | tf_op jit(solution)/shard_map/rhk,rtk->rht/dot_general | solution.py:16
  15.5 2.9 fusion.31
  18.4 10.4 %fusion.10 = bf16[8,8,512]{2,1,0:T(8,128)(2,1)S(1)} fusion(bf16[8,2048,576]{1,2,0:T(8,128)(2,1)} %param.12, f32[8,8,2048]{2,1,0:T(8,128)} %get-tuple-element.10, f32[8,8]{1,0:T(8,128)S(1)} %get-tuple-element.9), kind=kOutput, calls=%fused_computation.15 | convolution fusion | flops 134512640 | bytes 17367296 | tf_op jit(solution)/shard_map/rht,rtk->rhk/dot_general | solution.py:38
  28.9 0.3 fusion.14
  29.1 21.8 %all_gather.3 = bf16[128,1024]{1,0:T(8,128)(2,1)S(1)} all-gather(bf16[8,1024]{1,0:T(8,128)(2,1)S(1)} %fusion.14), channel_id=1, replica_groups=mesh['dp'=16,'tp'=16] {'dp'}, dimensions={0}, use_global_device_ids=true | all-gather | bytes 278528 | tf_op jit(solution)/shard_map/all_gather | solution.py:68
  51.0 2.3 convolution_convert_fusion.2
  53.2 0.0 all-reduce.4.cloned.1.call-update
  53.3 0.0 all-reduce.6.cloned.1.call-start
  53.3 0.1 copy.26
  53.5 136.2 %all-reduce.4.cloned.1.call-done = bf16[128,448]{1,0:T(8,128)(2,1)} async-done(((bf16[128,448]{1,0:T(8,128)(2,1)}), bf16[128,448]{1,0:T(8,128)(2,1)}) %all-reduce.4.cloned.1.call-update) | async-done | bytes 114704 | tf_op jit(solution)/shard_map/psum | solution.py:76
  189.7 1.0 fusion.23
  190.7 27.8 %psum.29 = f32[128]{0:T(128)S(1)} all-reduce(f32[128]{0:T(128)S(1)} %get-tuple-element.8), channel_id=1, replica_groups=mesh['dp'=16,'tp'=16] {'dp'}, use_global_device_ids=true, to_apply=%region_4.5 | all-reduce | flops 128 | bytes 1024 | tf_op jit(solution)/shard_map/psum | solution.py:79
  218.5 2.0 convolution_convert_fusion.1
  220.5 2.4 convolution_convert_fusion
  222.9 0.0 all-reduce.6.cloned.1.call-update
  222.9 0.0 reduce-scatter.4.cloned.1.call-start
  223.0 142.1 %all-reduce.6.cloned.1.call-done = (bf16[128,1152]{1,0:T(8,128)(2,1)}, bf16[128,1152]{1,0:T(8,128)(2,1)}) async-done(((bf16[128,1152]{1,0:T(8,128)(2,1)}, bf16[128,1152]{1,0:T(8,128)(2,1)}), (bf16[128,1152]{1,0:T(8,128)(2,1)}, bf16[128,1152]{1,0:T(8,128)(2,1)})) %all-reduce.6.cloned.1.call-update) | async-done | bytes 589840 | tf_op jit(solution)/shard_map/psum | solution.py:87
  365.0 2.5 convolution_convert_fusion.3
  367.6 0.0 reduce-scatter.4.cloned.1.call-update
  367.6 74.8 %reduce-scatter.4.cloned.1.call-done = bf16[8,448]{1,0:T(8,128)(2,1)} async-done(((bf16[128,448]{1,0:T(8,128)(2,1)}), bf16[8,448]{1,0:T(8,128)(2,1)}) %reduce-scatter.4.cloned.1.call-update) | async-done | bytes 7184 | tf_op jit(solution)/shard_map/reduce_scatter | solution.py:90
  442.4 1.3 add_convert_fusion.1
  (14 shorter events, 0.0 us)
Async XLA Ops:
  6.5 1.7 copy-start
  6.5 183.1 %all-reduce.4.cloned.1.call-start = ((), (), s32[]{:S(2)}) async-start(), calls=%async_computation.1 | async-start | bytes 262144 | tf_op jit(solution)/shard_map/psum | solution.py:76
  8.5 20.4 %copy-start.1 = (bf16[8,512,128]{2,1,0:T(8,128)(2,1)S(1)}, bf16[8,512,128]{2,1,0:T(8,128)(2,1)}, u32[]{:S(2)}) copy-start(bf16[8,512,128]{2,1,0:T(8,128)(2,1)} %param.15) | copy-start | bytes 3145732
  8.5 44.8 %copy-start.3 = (bf16[128,448]{0,1:T(8,128)(2,1)S(1)}, bf16[128,448]{0,1:T(8,128)(2,1)}, u32[]{:S(2)}) copy-start(bf16[128,448]{0,1:T(8,128)(2,1)} %param.17) | copy-start | bytes 344068
  8.5 45.0 %copy-start.4 = (bf16[448]{0:T(512)(128)(2,1)S(1)}, bf16[448]{0:T(512)(128)(2,1)}, u32[]{:S(2)}) copy-start(bf16[448]{0:T(512)(128)(2,1)} %param.18) | copy-start | bytes 2692
  18.4 200.1 %copy-start.2 = (bf16[448,1152]{1,0:T(8,128)(2,1)S(1)}, bf16[448,1152]{1,0:T(8,128)(2,1)}, u32[]{:S(2)}) copy-start(bf16[448,1152]{1,0:T(8,128)(2,1)} %param.19) | copy-start | bytes 3096580
  53.3 311.8 %all-reduce.6.cloned.1.call-start = ((), (), s32[]{:S(2)}) async-start(), calls=%async_computation.3 | async-start | bytes 1179648 | tf_op jit(solution)/shard_map/psum | solution.py:87
  222.9 219.5 %reduce-scatter.4.cloned.1.call-start = ((), (), s32[]{:S(2)}) async-start(), calls=%async_computation.2 | async-start | bytes 139264 | tf_op jit(solution)/shard_map/reduce_scatter | solution.py:90
Sparse Core Ops, SparseCore 0:
  53.4 136.2 all-reduce.3
  223.0 141.9 all-reduce.5
  367.7 74.6 reduce-scatter.3
where the time goes:
time: 451 us; the launch traced here: 450 us
  waiting for transfers between devices  353 us (78%)
  blocking collectives  49.6 us (11%)
  matrix products  30.1 us (7%)
  between operations  13.2 us (3%)
    psum x1, waiting for transfers between devices, on_device(): lax.psum(up.astype(jnp.bfloat16), 'dp').astype(jnp.float32)  142 us
    psum x1, waiting for transfers between devices, on_device(): lax.psum(partial_out.astype(jnp.bfloat16), 'tp').astype(jnp.float32)  136 us
    reduce_scatter x1, waiting for transfers between devices, on_device(): lax.psum_scatter(jnp.dot(hidden, w_down, preferred_element_type=jnp.float...  74.8 us
    psum x1, blocking collectives, on_device(): squares = lax.psum(squares, 'dp')  27.8 us
    all_gather x1, blocking collectives, on_device(): lax.all_gather(value_rows, 'dp', axis=0, tiled=True)  21.8 us
    dot_general x1, matrix products, attend(): jnp.einsum('rht,rtk->rhk', probs, latent_cache[:, :, :KVR], preferred_ele...  10.4 us
  transfers between devices with their start and end apart: 3, of which 3 were waited for; matrix products, arithmetic and copies ran while one was open for 0% of the time, Pallas kernels for 0%

commit v1 on v0

v1 whole, which is shorter than its diff:
```python
import functools

import jax
import jax.numpy as jnp
from jax import lax
from jax.experimental import pallas as pl
from jax.experimental.pallas import tpu as pltpu
from jax.sharding import PartitionSpec as P

MESH = pl.DeviceIdType.MESH
NOPE = 128
ROPE = 64
KVR = 512
VD = 128
CHUNK = 512
NT = (((1,), (1,)), ((), ()))


def attend_kernel(
    lengths,
    query,
    cache,
    w_uk,
    w_value,
    values,
    held,
    uk_held,
    value_held,
    queries,
    scores,
    top,
    total,
    context,
    cache_sem,
    weight_sem,
):
    requests, heads = queries.shape[0], queries.shape[1]
    uk_copy = pltpu.make_async_copy(w_uk, uk_held, weight_sem.at[0])
    value_copy = pltpu.make_async_copy(w_value, value_held, weight_sem.at[1])
    uk_copy.start()

    def chunk_copy(b, c):
        slots = pl.ds(pl.multiple_of(c * CHUNK, CHUNK), CHUNK)
        return pltpu.make_async_copy(
            cache.at[b, :, slots], held.at[b, :, slots], cache_sem.at[b, c]
        )

    chunks = [lax.div(lengths[b] + (CHUNK - 1), CHUNK) for b in range(requests)]
    for b in range(requests):
        chunk_copy(b, 0).start()
    for b in range(requests):
        pl.loop(1, chunks[b])(lambda c, b=b: chunk_copy(b, c).start())
    value_copy.start()

    uk_copy.wait()
    width = NOPE + ROPE
    for h in range(heads):
        nope = query[:, h * width : h * width + NOPE]
        queries[:, h, :KVR] = jnp.dot(nope, uk_held[h], preferred_element_type=jnp.float32)
        queries[:, h, KVR:] = query[:, h * width + NOPE : (h + 1) * width].astype(jnp.float32)

    scale = 1.0 / jnp.sqrt(jnp.float32(NOPE + ROPE))

    def chunk_scores(b, c):
        slots = pl.ds(pl.multiple_of(c * CHUNK, CHUNK), CHUNK)
        got = jnp.dot(
            queries[b].astype(jnp.bfloat16),
            held[b, :, slots],
            preferred_element_type=jnp.float32,
        )
        at = c * CHUNK + lax.broadcasted_iota(jnp.int32, got.shape, 1)
        got = jnp.where(at < lengths[b], got * scale, -jnp.inf)
        scores[b, :, slots] = got
        return jnp.max(got, axis=1, keepdims=True)

    for b in range(requests):
        chunk_copy(b, 0).wait()
        top[b] = jnp.broadcast_to(chunk_scores(b, 0), top.shape[1:])
    for b in range(requests):

        @pl.loop(1, chunks[b])
        def _(c, b=b):
            chunk_copy(b, c).wait()
            top[b] = jnp.maximum(top[b], chunk_scores(b, c))

    def chunk_context(b, c):
        slots = pl.ds(pl.multiple_of(c * CHUNK, CHUNK), CHUNK)
        probs = jnp.exp(scores[b, :, slots] - top[b, :, :1])
        part = lax.dot_general(
            probs.astype(jnp.bfloat16),
            held[b, :KVR, slots],
            NT,
            preferred_element_type=jnp.float32,
        )
        return part, jnp.sum(probs, axis=1, keepdims=True)

    for b in range(requests):
        part, sums = chunk_context(b, 0)
        context[:, b, :] = part
        total[b] = jnp.broadcast_to(sums, total.shape[1:])
    for b in range(requests):

        @pl.loop(1, chunks[b])
        def _(c, b=b):
            part, sums = chunk_context(b, c)
            context[:, b, :] += part
            total[b] += sums

    for b in range(requests):
        context[:, b, :] = context[:, b, :] / total[b, :, :1]
    value_copy.wait()
    for h in range(heads):
        values[:, h * VD : (h + 1) * VD] = jnp.dot(
            context[h].astype(jnp.bfloat16), value_held[h], preferred_element_type=jnp.float32
        ).astype(jnp.bfloat16)


def attend(query, cache, lengths, w_uk, w_value):
    requests, depth, slots = cache.shape
    heads = w_uk.shape[0]
    vmem = pl.BlockSpec(memory_space=pltpu.VMEM)
    anywhere = pl.BlockSpec(memory_space=pl.ANY)
    return pl.pallas_call(
        attend_kernel,
        out_shape=jax.ShapeDtypeStruct((requests, heads * VD), jnp.bfloat16),
        in_specs=[pl.BlockSpec(memory_space=pltpu.SMEM), vmem, anywhere, anywhere, anywhere],
        out_specs=vmem,
        scratch_shapes=[
            pltpu.VMEM(cache.shape, jnp.bfloat16),
            pltpu.VMEM(w_uk.shape, jnp.bfloat16),
            pltpu.VMEM(w_value.shape, jnp.bfloat16),
            pltpu.VMEM((requests, heads, depth), jnp.float32),
            pltpu.VMEM((requests, heads, slots), jnp.float32),
            pltpu.VMEM((requests, heads, 128), jnp.float32),
            pltpu.VMEM((requests, heads, 128), jnp.float32),
            pltpu.VMEM((heads, requests, KVR), jnp.float32),
            pltpu.SemaphoreType.DMA((requests, slots // CHUNK)),
            pltpu.SemaphoreType.DMA((2,)),
        ],
        compiler_params=pltpu.CompilerParams(vmem_limit_bytes=40 * 2**20),
        name="attend",
    )(lengths, query, cache, w_uk, w_value)


def layer_kernel(
    model,
    values,
    w_out,
    residual,
    gain,
    w_gate,
    w_up,
    w_down,
    mixed,
    out_held,
    gate_held,
    up_held,
    down_held,
    residual_held,
    residual_rows,
    all_values,
    out_send,
    out_recv,
    stream_rows,
    mlp_send,
    mlp_recv,
    hidden_rows,
    down_send,
    down_recv,
    weight_sem,
    send_sem,
    recv_sem,
):
    dp, tp = lax.axis_index("dp"), lax.axis_index("tp")
    groups = all_values.shape[0]
    rows = values.shape[0]
    columns = mixed.shape[1]
    units = gate_held.shape[1]
    wide = out_send.shape[2]

    loads = [
        pltpu.make_async_copy(src, dst, weight_sem.at[at])
        for at, (src, dst) in enumerate(
            [
                (w_out, out_held),
                (residual, residual_held),
                (w_gate, gate_held),
                (w_up, up_held),
                (w_down, down_held),
            ]
        )
    ]
    for load in loads:
        load.start()

    def peer(axis, d):
        me = dp if axis == "dp" else tp
        return lax.rem(me + d, groups)

    barrier = pltpu.get_barrier_semaphore()
    for axis in ("dp", "tp"):

        @pl.loop(1, groups)
        def _(d, axis=axis):
            pl.semaphore_signal(
                barrier, inc=1, device_id={axis: peer(axis, d)}, device_id_type=MESH
            )

    pl.semaphore_wait(barrier, 2 * (groups - 1))

    def exchange(axis, phase, source, target):
        me = dp if axis == "dp" else tp

        def copy(d):
            to = peer(axis, d)
            return pltpu.make_async_remote_copy(
                src_ref=source(to),
                dst_ref=target.at[me],
                send_sem=send_sem.at[phase, to],
                recv_sem=recv_sem.at[phase, me],
                device_id={axis: to},
                device_id_type=MESH,
            )

        @pl.loop(1, groups)
        def _(d):
            copy(d).start()

        def arrive():
            @pl.loop(1, groups)
            def _(d):
                whence = peer(axis, d)
                pltpu.make_async_remote_copy(
                    src_ref=source(whence),
                    dst_ref=target.at[whence],
                    send_sem=send_sem.at[phase, whence],
                    recv_sem=recv_sem.at[phase, whence],
                    device_id={axis: whence},
                    device_id_type=MESH,
                ).wait_recv()

        def sent():
            @pl.loop(1, groups)
            def _(d):
                copy(d).wait_send()

        return arrive, sent

    finish = []

    arrive, sent = exchange("dp", 0, lambda to: values, all_values)
    finish.append(sent)
    all_values[dp] = values[...]
    loads[1].wait()
    residual_rows[...] = residual_held[...].astype(jnp.float32).T
    loads[0].wait()
    arrive()
    attended = lax.dot_general(
        all_values[...].reshape(groups * rows, -1),
        out_held[...],
        NT,
        preferred_element_type=jnp.float32,
    )
    out_send[:, :, :columns] = attended.astype(jnp.bfloat16).reshape(groups, rows, columns)

    arrive, sent = exchange("tp", 1, lambda to: out_send.at[to], out_recv)
    finish.append(sent)
    out_recv[tp] = out_send[tp]
    arrive()
    own = residual_rows[pl.ds(pl.multiple_of(tp * rows, rows), rows), :]
    own = own + jnp.sum(out_recv[:, :, :columns].astype(jnp.float32), axis=0)
    own = own.astype(jnp.bfloat16)
    stream_rows[tp, :, :columns] = own

    arrive, sent = exchange("tp", 2, lambda to: stream_rows.at[tp], stream_rows)
    finish.append(sent)
    loads[2].wait()
    loads[3].wait()
    arrive()
    stream = stream_rows[:, :, :columns].astype(jnp.float32).reshape(groups * rows, columns)
    squares = jnp.sum(stream * stream, axis=1, keepdims=True)
    scaled = (stream * gain[...].astype(jnp.float32)).astype(jnp.bfloat16)
    gate = jnp.dot(scaled, gate_held[...], preferred_element_type=jnp.float32)
    mlp_send[:, :, :units] = gate.astype(jnp.bfloat16).reshape(groups, rows, units)
    up = jnp.dot(scaled, up_held[...], preferred_element_type=jnp.float32)
    mlp_send[:, :, units : 2 * units] = up.astype(jnp.bfloat16).reshape(groups, rows, units)
    high = squares.astype(jnp.bfloat16).astype(jnp.float32)
    lane = lax.broadcasted_iota(jnp.int32, (groups * rows, 128), 1)
    split = jnp.where(lane == 0, high, jnp.where(lane == 1, squares - high, 0.0))
    mlp_send[:, :, 2 * units :] = split.astype(jnp.bfloat16).reshape(groups, rows, 128)

    arrive, sent = exchange("dp", 3, lambda to: mlp_send.at[to], mlp_recv)
    finish.append(sent)
    mlp_recv[dp] = mlp_send[dp]
    arrive()
    sums = jnp.sum(mlp_recv[...].astype(jnp.float32), axis=0)
    squares = sums[:, 2 * units : 2 * units + 1] + sums[:, 2 * units + 1 : 2 * units + 2]
    inv_rms = 1.0 / jnp.sqrt(squares / model + 1e-06)
    gate = sums[:, :units] * inv_rms
    up = sums[:, units : 2 * units] * inv_rms
    hidden = gate / (1.0 + jnp.exp(-gate)) * up
    hidden_rows[dp] = hidden.astype(jnp.bfloat16)

    arrive, sent = exchange("dp", 4, lambda to: hidden_rows.at[dp], hidden_rows)
    finish.append(sent)
    loads[4].wait()
    arrive()
    down = lax.dot_general(
        hidden_rows[...].reshape(groups * rows, units),
        down_held[...],
        NT,
        preferred_element_type=jnp.float32,
    )
    down_send[:, :, :columns] = down.astype(jnp.bfloat16).reshape(groups, rows, columns)

    arrive, sent = exchange("tp", 5, lambda to: down_send.at[to], down_recv)
    finish.append(sent)
    down_recv[tp] = down_send[tp]
    arrive()
    result = jnp.sum(down_recv[:, :, :columns].astype(jnp.float32), axis=0)
    mixed[...] = (own.astype(jnp.float32) + result).astype(jnp.bfloat16)
    for sent in finish:
        sent()


def layer(values, w_out, residual, gain, w_gate, w_up, w_down, groups, model):
    rows, depth = values.shape
    columns, units = w_down.shape
    wide = -(-columns // 128) * 128
    vmem = pl.BlockSpec(memory_space=pltpu.VMEM)
    anywhere = pl.BlockSpec(memory_space=pl.ANY)
    blocks = lambda width: pltpu.VMEM((groups, rows, width), jnp.bfloat16)
    return pl.pallas_call(
        functools.partial(layer_kernel, model),
        out_shape=jax.ShapeDtypeStruct((rows, columns), jnp.bfloat16),
        in_specs=[vmem, anywhere, anywhere, vmem, anywhere, anywhere, anywhere],
        out_specs=vmem,
        scratch_shapes=[
            pltpu.VMEM(w_out.shape, jnp.bfloat16),
            pltpu.VMEM(w_gate.shape, jnp.bfloat16),
            pltpu.VMEM(w_up.shape, jnp.bfloat16),
            pltpu.VMEM(w_down.shape, jnp.bfloat16),
            pltpu.VMEM(residual.shape, jnp.bfloat16),
            pltpu.VMEM(residual.shape[::-1], jnp.float32),
            blocks(depth),
            blocks(wide),
            blocks(wide),
            blocks(wide),
            blocks(2 * units + 128),
            blocks(2 * units + 128),
            blocks(units),
            blocks(wide),
            blocks(wide),
            pltpu.SemaphoreType.DMA((5,)),
            pltpu.SemaphoreType.DMA((6, groups)),
            pltpu.SemaphoreType.DMA((6, groups)),
        ],
        compiler_params=pltpu.CompilerParams(
            collective_id=0, has_side_effects=True, vmem_limit_bytes=40 * 2**20
        ),
        name="layer",
    )(values, w_out, residual, gain, w_gate, w_up, w_down)


def solution(mesh):
    groups = mesh.shape["dp"]

    def on_device(
        query,
        latent_cache,
        lengths,
        w_uk,
        value_up_weight,
        w_out,
        residual,
        mlp_norm_scale,
        w_gate,
        w_up,
        w_down,
    ):
        values = attend(query, jnp.swapaxes(latent_cache, 1, 2), lengths, w_uk, value_up_weight)
        return layer(
            values,
            w_out.T,
            residual.T,
            mlp_norm_scale[None, :],
            w_gate,
            w_up,
            w_down.T,
            groups,
            groups * mlp_norm_scale.shape[0],
        )

    return jax.shard_map(
        on_device,
        mesh=mesh,
        in_specs=(
            P("dp", "tp"),
            P("dp", None, None),
            P("dp"),
            P("tp", None, None),
            P("tp", None, None),
            P("tp", "dp"),
            P(None, "dp"),
            P("dp"),
            P("dp", "tp"),
            P("dp", "tp"),
            P("tp", "dp"),
        ),
        out_specs=P("tp", "dp"),
        check_vma=False,
    )
```

time: 451 us -> 68.4 us (0.15)
  the two profiles are of different devices: /device:TPU:8 before, /device:TPU:1 now
where the time goes in v1:
time: 68.4 us; the launch traced here: 68.1 us
  Pallas kernels  62.8 us (92%)
  local copies, waits for them, and re-layouts  5.14 us (8%)
    pallas_call x1, Pallas kernels, layer(): pl.pallas_call(functools.partial(layer_kernel, model), out_shape=jax.Shap...  56.7 us
    pallas_call x1, Pallas kernels, attend(): pl.pallas_call(attend_kernel, out_shape=jax.ShapeDtypeStruct((requests, h...  6.09 us
    unnamed x19, local copies, waits for them, and re-layouts  4.46 us

profile of v1, /device:TPU:1, one launch (start us, length us, event | category | flops | bytes accessed | tf_op | source)
XLA Modules:
  0.0 68.1 jit_solution(2712346822048649343)
XLA Ops:
  0.0 0.7 %broadcast_in_dim.3.gain = bf16[1,448]{1,0:T(2,128)(2,1)S(1)} reshape(bf16[448]{0:T(512)(128)(2,1)} %param.18) | data formatting | bytes 1792 | tf_op jit(solution)/shard_map/broadcast_in_dim | solution.py:386
  0.7 0.0 copy-start
  0.7 1.2 %copy-done = bf16[8,128,512]{2,1,0:T(8,128)(2,1)S(1)} copy-done((bf16[8,128,512]{2,1,0:T(8,128)(2,1)S(1)}, bf16[8,128,512]{2,1,0:T(8,128)(2,1)}, u32[]{:S(2)}) %copy-start) | copy-done | bytes 1048600
  1.9 0.0 copy-start.1
  1.9 1.2 %copy-done.1 = bf16[8,512,128]{2,1,0:T(8,128)(2,1)S(1)} copy-done((bf16[8,512,128]{2,1,0:T(8,128)(2,1)S(1)}, bf16[8,512,128]{2,1,0:T(8,128)(2,1)}, u32[]{:S(2)}) %copy-start.1) | copy-done | bytes 1048600
  3.1 0.0 copy-start.7
  3.1 0.7 %copy-done.7 = bf16[8,1536]{1,0:T(8,128)(2,1)S(1)} copy-done((bf16[8,1536]{1,0:T(8,128)(2,1)S(1)}, bf16[8,1536]{1,0:T(8,128)(2,1)}, u32[]{:S(2)}) %copy-start.7) | copy-done | bytes 24600
  3.9 0.0 copy-start.8
  3.9 0.7 copy-done.8
  4.5 0.0 copy-start.2
  4.5 0.0 copy-start.3
  4.5 0.0 copy-start.4
  4.5 0.0 copy-start.5
  4.5 0.0 copy-start.6
  4.5 6.1 %attend.1.values = bf16[8,1024]{1,0:T(8,128)(2,1)S(1)} custom-call(s32[8]{0:T(128)S(1)} %copy-done.8, bf16[8,1536]{1,0:T(8,128)(2,1)S(1)} %copy-done.7, bf16[8,576,2048]{2,1,0:T(8,128)(2,1)} %bitcast.7, bf16[8,128,512]{2,1,0:T(8,128)(2,1)S(1)} %copy-done, bf16[8,512,128]{2,1,0:T(8,128)(2,1)S(1)} %copy-done.1), custom_call_target="tpu_custom_call" | custom-call | tf_op jit(solution)/shard_map/attend/pallas_call | solution.py:123
  10.6 0.0 copy-done.2
  10.7 0.0 copy-done.3
  10.7 0.0 copy-done.4
  10.7 0.0 copy-done.5
  10.7 0.0 copy-done.6
  10.7 56.7 %layer.1 = bf16[8,448]{1,0:T(8,128)(2,1)S(1)} custom-call(bf16[8,1024]{1,0:T(8,128)(2,1)S(1)} %attend.1.values, bf16[448,1024]{1,0:T(8,128)(2,1)S(1)} %bitcast.5, bf16[448,128]{1,0:T(8,128)(2,1)S(1)} %bitcast.6, bf16[1,448]{1,0:T(2,128)(2,1)S(1)} %broadcast_in_dim.3.gain, bf16[448,1152]{1,0:T(8,128)(2,1)S(1)} %copy-done.2, bf16[448,1152]{1,0:T(8,128)(2,1)S(1)} %copy-done.3, ...), custom_call_target="tpu_custom_call" | custom-call | tf_op jit(solution)/shard_map/layer/pallas_call | solution.py:333
  67.5 0.6 copy.13
Async XLA Ops:
  0.7 1.2 %copy-start = (bf16[8,128,512]{2,1,0:T(8,128)(2,1)S(1)}, bf16[8,128,512]{2,1,0:T(8,128)(2,1)}, u32[]{:S(2)}) copy-start(bf16[8,128,512]{2,1,0:T(8,128)(2,1)} %w_uk.1) | copy-start | bytes 3145732
  1.9 1.2 %copy-start.1 = (bf16[8,512,128]{2,1,0:T(8,128)(2,1)S(1)}, bf16[8,512,128]{2,1,0:T(8,128)(2,1)}, u32[]{:S(2)}) copy-start(bf16[8,512,128]{2,1,0:T(8,128)(2,1)} %w_value.1) | copy-start | bytes 3145732
  3.1 0.7 %copy-start.7 = (bf16[8,1536]{1,0:T(8,128)(2,1)S(1)}, bf16[8,1536]{1,0:T(8,128)(2,1)}, u32[]{:S(2)}) copy-start(bf16[8,1536]{1,0:T(8,128)(2,1)} %query.1) | copy-start | bytes 73732
  3.9 0.7 copy-start.8
  4.5 6.1 %copy-start.2 = (bf16[448,1152]{1,0:T(8,128)(2,1)S(1)}, bf16[448,1152]{1,0:T(8,128)(2,1)}, u32[]{:S(2)}) copy-start(bf16[448,1152]{1,0:T(8,128)(2,1)} %w_gate.1) | copy-start | bytes 3096580
  4.5 6.1 %copy-start.3 = (bf16[448,1152]{1,0:T(8,128)(2,1)S(1)}, bf16[448,1152]{1,0:T(8,128)(2,1)}, u32[]{:S(2)}) copy-start(bf16[448,1152]{1,0:T(8,128)(2,1)} %w_up.1) | copy-start | bytes 3096580
  4.5 6.1 %copy-start.4 = (bf16[1152,448]{0,1:T(8,128)(2,1)S(1)}, bf16[1152,448]{0,1:T(8,128)(2,1)}, u32[]{:S(2)}) copy-start(bf16[1152,448]{0,1:T(8,128)(2,1)} %param.21) | copy-start | bytes 3096580
  4.5 6.1 %copy-start.5 = (bf16[1024,448]{0,1:T(8,128)(2,1)S(1)}, bf16[1024,448]{0,1:T(8,128)(2,1)}, u32[]{:S(2)}) copy-start(bf16[1024,448]{0,1:T(8,128)(2,1)} %param.16) | copy-start | bytes 2752516
  4.5 6.1 %copy-start.6 = (bf16[128,448]{0,1:T(8,128)(2,1)S(1)}, bf16[128,448]{0,1:T(8,128)(2,1)}, u32[]{:S(2)}) copy-start(bf16[128,448]{0,1:T(8,128)(2,1)} %param.17) | copy-start | bytes 344068

commit v2 on v1

--- a/solution.py
+++ b/solution.py
@@ -7,22 +7,34 @@
 from jax.experimental.pallas import tpu as pltpu
 from jax.sharding import PartitionSpec as P
 
+DP_PEERS = sorted(
+    [(a, b, c) for a in range(2) for b in range(4) for c in range(2) if a + b + c],
+    key=lambda d: -(2 * d[0] + min(d[1], 4 - d[1])),
+)
+CHIP_PEERS = [d for d in DP_PEERS if d[2] == 0]
+TP_PEERS = sorted(
+    [(a, b) for a in range(8) for b in range(2) if a + b],
+    key=lambda d: -(min(d[0], 8 - d[0]) + d[1]),
+)
 MESH = pl.DeviceIdType.MESH
 NOPE = 128
 ROPE = 64
 KVR = 512
 VD = 128
 CHUNK = 512
+VMEM_BYTES = 60 * 2**20
 NT = (((1,), (1,)), ((), ()))
 
 
 def attend_kernel(
-    lengths,
-    query,
+    lengths_in,
+    query_in,
     cache,
     w_uk,
     w_value,
     values,
+    lengths,
+    query,
     held,
     uk_held,
     value_held,
@@ -37,6 +49,10 @@
     requests, heads = queries.shape[0], queries.shape[1]
     uk_copy = pltpu.make_async_copy(w_uk, uk_held, weight_sem.at[0])
     value_copy = pltpu.make_async_copy(w_value, value_held, weight_sem.at[1])
+    lengths_copy = pltpu.make_async_copy(lengths_in, lengths, weight_sem.at[2])
+    query_copy = pltpu.make_async_copy(query_in, query, weight_sem.at[3])
+    lengths_copy.start()
+    query_copy.start()
     uk_copy.start()
 
     def chunk_copy(b, c):
@@ -45,13 +61,15 @@
             cache.at[b, :, slots], held.at[b, :, slots], cache_sem.at[b, c]
         )
 
+    for b in range(requests):
+        chunk_copy(b, 0).start()
+    lengths_copy.wait()
     chunks = [lax.div(lengths[b] + (CHUNK - 1), CHUNK) for b in range(requests)]
-    for b in range(requests):
-        chunk_copy(b, 0).start()
     for b in range(requests):
         pl.loop(1, chunks[b])(lambda c, b=b: chunk_copy(b, c).start())
     value_copy.start()
 
+    query_copy.wait()
     uk_copy.wait()
     width = NOPE + ROPE
     for h in range(heads):
@@ -123,9 +141,11 @@
     return pl.pallas_call(
         attend_kernel,
         out_shape=jax.ShapeDtypeStruct((requests, heads * VD), jnp.bfloat16),
-        in_specs=[pl.BlockSpec(memory_space=pltpu.SMEM), vmem, anywhere, anywhere, anywhere],
+        in_specs=[anywhere] * 5,
         out_specs=vmem,
         scratch_shapes=[
+            pltpu.SMEM(lengths.shape, jnp.int32),
+            pltpu.VMEM(query.shape, jnp.bfloat16),
             pltpu.VMEM(cache.shape, jnp.bfloat16),
             pltpu.VMEM(w_uk.shape, jnp.bfloat16),
             pltpu.VMEM(w_value.shape, jnp.bfloat16),
@@ -135,9 +155,9 @@
             pltpu.VMEM((requests, heads, 128), jnp.float32),
             pltpu.VMEM((heads, requests, KVR), jnp.float32),
             pltpu.SemaphoreType.DMA((requests, slots // CHUNK)),
-            pltpu.SemaphoreType.DMA((2,)),
+            pltpu.SemaphoreType.DMA((4,)),
         ],
-        compiler_params=pltpu.CompilerParams(vmem_limit_bytes=40 * 2**20),
+        compiler_params=pltpu.CompilerParams(vmem_limit_bytes=VMEM_BYTES),
         name="attend",
     )(lengths, query, cache, w_uk, w_value)
 
@@ -147,7 +167,7 @@
     values,
     w_out,
     residual,
-    gain,
+    gain_in,
     w_gate,
     w_up,
     w_down,
@@ -157,13 +177,20 @@
     up_held,
     down_held,
     residual_held,
+    gain,
     residual_rows,
     all_values,
     out_send,
     out_recv,
     stream_rows,
-    mlp_send,
-    mlp_recv,
+    gate_pair,
+    gate_other,
+    gate_send,
+    gate_recv,
+    up_pair,
+    up_other,
+    up_send,
+    up_recv,
     hidden_rows,
     down_send,
     down_recv,
@@ -176,7 +203,6 @@
     rows = values.shape[0]
     columns = mixed.shape[1]
     units = gate_held.shape[1]
-    wide = out_send.shape[2]
 
     loads = [
         pltpu.make_async_copy(src, dst, weight_sem.at[at])
@@ -184,6 +210,7 @@
             [
                 (w_out, out_held),
                 (residual, residual_held),
+                (gain_in, gain),
                 (w_gate, gate_held),
                 (w_up, up_held),
                 (w_down, down_held),
@@ -193,63 +220,42 @@
     for load in loads:
         load.start()
 
+    core, y, x_hi = lax.rem(dp, 2), lax.rem(dp // 2, 4), dp // 8
+    x_lo, z = lax.rem(tp, 2), tp // 2
+
     def peer(axis, d):
-        me = dp if axis == "dp" else tp
-        return lax.rem(me + d, groups)
+        if axis == "dp":
+            return (
+                lax.rem(x_hi + d[0], 2) * 8 + lax.rem(y + d[1], 4) * 2 + lax.rem(core + d[2], 2)
+            )
+        return lax.rem(z + d[0], 8) * 2 + lax.rem(x_lo + d[1], 2)
 
     barrier = pltpu.get_barrier_semaphore()
-    for axis in ("dp", "tp"):
-
-        @pl.loop(1, groups)
-        def _(d, axis=axis):
+    for axis, peers in (("dp", DP_PEERS), ("tp", TP_PEERS)):
+        for d in peers:
             pl.semaphore_signal(
                 barrier, inc=1, device_id={axis: peer(axis, d)}, device_id_type=MESH
             )
-
-    pl.semaphore_wait(barrier, 2 * (groups - 1))
-
-    def exchange(axis, phase, source, target):
-        me = dp if axis == "dp" else tp
-
-        def copy(d):
+    pl.semaphore_wait(barrier, len(DP_PEERS) + len(TP_PEERS))
+
+    finish = []
+
+    def exchange(axis, phase, peers, source, target, place):
+        for d in peers:
             to = peer(axis, d)
-            return pltpu.make_async_remote_copy(
+            pltpu.make_async_remote_copy(
                 src_ref=source(to),
-                dst_ref=target.at[me],
-                send_sem=send_sem.at[phase, to],
-                recv_sem=recv_sem.at[phase, me],
+                dst_ref=target.at[place],
+                send_sem=send_sem.at[phase],
+                recv_sem=recv_sem.at[phase],
                 device_id={axis: to},
                 device_id_type=MESH,
-            )
-
-        @pl.loop(1, groups)
-        def _(d):
-            copy(d).start()
-
-        def arrive():
-            @pl.loop(1, groups)
-            def _(d):
-                whence = peer(axis, d)
-                pltpu.make_async_remote_copy(
-                    src_ref=source(whence),
-                    dst_ref=target.at[whence],
-                    send_sem=send_sem.at[phase, whence],
-                    recv_sem=recv_sem.at[phase, whence],
-                    device_id={axis: whence},
-                    device_id_type=MESH,
-                ).wait_recv()
-
-        def sent():
-            @pl.loop(1, groups)
-            def _(d):
-                copy(d).wait_send()
-
-        return arrive, sent
-
-    finish = []
-
-    arrive, sent = exchange("dp", 0, lambda to: values, all_values)
-    finish.append(sent)
+            ).start()
+        blocks = target.at[: len(peers)]
+        finish.append(pltpu.make_async_copy(blocks, blocks, send_sem.at[phase]).wait)
+        return pltpu.make_async_copy(blocks, blocks, recv_sem.at[phase]).wait
+
+    arrive = exchange("dp", 0, DP_PEERS, lambda to: values, all_values, dp)
     all_values[dp] = values[...]
     loads[1].wait()
     residual_rows[...] = residual_held[...].astype(jnp.float32).T
@@ -263,8 +269,7 @@
     )
     out_send[:, :, :columns] = attended.astype(jnp.bfloat16).reshape(groups, rows, columns)
 
-    arrive, sent = exchange("tp", 1, lambda to: out_send.at[to], out_recv)
-    finish.append(sent)
+    arrive = exchange("tp", 1, TP_PEERS, lambda to: out_send.at[to], out_recv, tp)
     out_recv[tp] = out_send[tp]
     arrive()
     own = residual_rows[pl.ds(pl.multiple_of(tp * rows, rows), rows), :]
@@ -272,38 +277,66 @@
     own = own.astype(jnp.bfloat16)
     stream_rows[tp, :, :columns] = own
 
-    arrive, sent = exchange("tp", 2, lambda to: stream_rows.at[tp], stream_rows)
-    finish.append(sent)
+    arrive = exchange("tp", 2, TP_PEERS, lambda to: stream_rows.at[tp], stream_rows, tp)
     loads[2].wait()
     loads[3].wait()
+    loads[4].wait()
     arrive()
     stream = stream_rows[:, :, :columns].astype(jnp.float32).reshape(groups * rows, columns)
     squares = jnp.sum(stream * stream, axis=1, keepdims=True)
-    scaled = (stream * gain[...].astype(jnp.float32)).astype(jnp.bfloat16)
-    gate = jnp.dot(scaled, gate_held[...], preferred_element_type=jnp.float32)
-    mlp_send[:, :, :units] = gate.astype(jnp.bfloat16).reshape(groups, rows, units)
-    up = jnp.dot(scaled, up_held[...], preferred_element_type=jnp.float32)
-    mlp_send[:, :, units : 2 * units] = up.astype(jnp.bfloat16).reshape(groups, rows, units)
+    scaled = (stream * gain[...].astype(jnp.float32)[None, :]).astype(jnp.bfloat16)
     high = squares.astype(jnp.bfloat16).astype(jnp.float32)
     lane = lax.broadcasted_iota(jnp.int32, (groups * rows, 128), 1)
     split = jnp.where(lane == 0, high, jnp.where(lane == 1, squares - high, 0.0))
-    mlp_send[:, :, 2 * units :] = split.astype(jnp.bfloat16).reshape(groups, rows, 128)
-
-    arrive, sent = exchange("dp", 3, lambda to: mlp_send.at[to], mlp_recv)
-    finish.append(sent)
-    mlp_recv[dp] = mlp_send[dp]
-    arrive()
-    sums = jnp.sum(mlp_recv[...].astype(jnp.float32), axis=0)
-    squares = sums[:, 2 * units : 2 * units + 1] + sums[:, 2 * units + 1 : 2 * units + 2]
+
+    def swap(part, wide, pair_send, pair_recv):
+        chips = groups // 2
+        blocks = wide.astype(jnp.bfloat16).reshape(chips, 2, rows, -1)
+        pair_send[0] = blocks[:, 0]
+        pair_send[1] = blocks[:, 1]
+        copy = pltpu.make_async_remote_copy(
+            src_ref=pair_send.at[1 - core],
+            dst_ref=pair_recv,
+            send_sem=send_sem.at[5 + part],
+            recv_sem=recv_sem.at[5 + part],
+            device_id={"dp": peer("dp", (0, 0, 1))},
+            device_id_type=MESH,
+        )
+        copy.start()
+        return copy
+
+    gate = jnp.dot(scaled, gate_held[...], preferred_element_type=jnp.float32)
+    gate_copy = swap(0, gate, gate_pair, gate_other)
+    up = jnp.dot(scaled, up_held[...], preferred_element_type=jnp.float32)
+    up = jnp.concatenate([up, split], axis=1)
+    up_copy = swap(1, up, up_pair, up_other)
+
+    def scatter(part, copy, pair_send, pair_recv, send, recv):
+        copy.wait_recv()
+        finish.append(copy.wait_send)
+        both = pair_send[core].astype(jnp.float32) + pair_recv[...].astype(jnp.float32)
+        send[...] = both.astype(jnp.bfloat16)
+        arrive = exchange(
+            "dp", 7 + part, CHIP_PEERS, lambda to: send.at[to // 2], recv, dp // 2
+        )
+        recv[dp // 2] = send[dp // 2]
+        return arrive
+
+    gate_arrive = scatter(0, gate_copy, gate_pair, gate_other, gate_send, gate_recv)
+    up_arrive = scatter(1, up_copy, up_pair, up_other, up_send, up_recv)
+    gate_arrive()
+    gate = jnp.sum(gate_recv[...].astype(jnp.float32), axis=0)
+    up_arrive()
+    up = jnp.sum(up_recv[...].astype(jnp.float32), axis=0)
+    squares = up[:, units : units + 1] + up[:, units + 1 : units + 2]
     inv_rms = 1.0 / jnp.sqrt(squares / model + 1e-06)
-    gate = sums[:, :units] * inv_rms
-    up = sums[:, units : 2 * units] * inv_rms
+    gate = gate * inv_rms
+    up = up[:, :units] * inv_rms
     hidden = gate / (1.0 + jnp.exp(-gate)) * up
     hidden_rows[dp] = hidden.astype(jnp.bfloat16)
 
-    arrive, sent = exchange("dp", 4, lambda to: hidden_rows.at[dp], hidden_rows)
-    finish.append(sent)
-    loads[4].wait()
+    arrive = exchange("dp", 3, DP_PEERS, lambda to: hidden_rows.at[dp], hidden_rows, dp)
+    loads[5].wait()
     arrive()
     down = lax.dot_general(
         hidden_rows[...].reshape(groups * rows, units),
@@ -313,8 +346,7 @@
     )
     down_send[:, :, :columns] = down.astype(jnp.bfloat16).reshape(groups, rows, columns)
 
-    arrive, sent = exchange("tp", 5, lambda to: down_send.at[to], down_recv)
-    finish.append(sent)
+    arrive = exchange("tp", 4, TP_PEERS, lambda to: down_send.at[to], down_recv, tp)
     down_recv[tp] = down_send[tp]
     arrive()
     result = jnp.sum(down_recv[:, :, :columns].astype(jnp.float32), axis=0)
@@ -330,10 +362,12 @@
     vmem = pl.BlockSpec(memory_space=pltpu.VMEM)
     anywhere = pl.BlockSpec(memory_space=pl.ANY)
     blocks = lambda width: pltpu.VMEM((groups, rows, width), jnp.bfloat16)
+    half = lambda width: pltpu.VMEM((groups // 2, rows, width), jnp.bfloat16)
+    pair = lambda width: pltpu.VMEM((2, groups // 2, rows, width), jnp.bfloat16)
     return pl.pallas_call(
         functools.partial(layer_kernel, model),
         out_shape=jax.ShapeDtypeStruct((rows, columns), jnp.bfloat16),
-        in_specs=[vmem, anywhere, anywhere, vmem, anywhere, anywhere, anywhere],
+        in_specs=[vmem] + [anywhere] * 6,
         out_specs=vmem,
         scratch_shapes=[
             pltpu.VMEM(w_out.shape, jnp.bfloat16),
@@ -341,22 +375,29 @@
             pltpu.VMEM(w_up.shape, jnp.bfloat16),
             pltpu.VMEM(w_down.shape, jnp.bfloat16),
             pltpu.VMEM(residual.shape, jnp.bfloat16),
+            pltpu.VMEM(gain.shape, jnp.bfloat16),
             pltpu.VMEM(residual.shape[::-1], jnp.float32),
             blocks(depth),
             blocks(wide),
             blocks(wide),
             blocks(wide),
-            blocks(2 * units + 128),
-            blocks(2 * units + 128),
+            pair(units),
+            half(units),
+            half(units),
+            half(units),
+            pair(units + 128),
+            half(units + 128),
+            half(units + 128),
+            half(units + 128),
             blocks(units),
             blocks(wide),
             blocks(wide),
-            pltpu.SemaphoreType.DMA((5,)),
-            pltpu.SemaphoreType.DMA((6, groups)),
-            pltpu.SemaphoreType.DMA((6, groups)),
+            pltpu.SemaphoreType.DMA((6,)),
+            pltpu.SemaphoreType.DMA((9,)),
+            pltpu.SemaphoreType.DMA((9,)),
         ],
         compiler_params=pltpu.CompilerParams(
-            collective_id=0, has_side_effects=True, vmem_limit_bytes=40 * 2**20
+            collective_id=0, has_side_effects=True, vmem_limit_bytes=VMEM_BYTES
         ),
         name="layer",
     )(values, w_out, residual, gain, w_gate, w_up, w_down)
@@ -383,7 +424,7 @@
             values,
             w_out.T,
             residual.T,
-            mlp_norm_scale[None, :],
+            mlp_norm_scale,
             w_gate,
             w_up,
             w_down.T,

time: 68.4 us -> 59 us (0.86)
  Pallas kernels: 62.8 us -> 57.4 us
  local copies, waits for them, and re-layouts: 5.14 us -> 1.3 us
    pallas_call x1, Pallas kernels: 56.7 us -> 48.3 us  [layer(): pl.pallas_call(functools.partial(layer_kernel, model), out_shape=jax.Shap...]
    unnamed x19 -> x1, local copies, waits for them, and re-layouts: 4.46 us -> 1.3 us
    pallas_call x1, Pallas kernels: 6.09 us -> 9.13 us  [attend(): pl.pallas_call(attend_kernel, out_shape=jax.ShapeDtypeStruct((requests, h...]
where the time goes in v2:
time: 59 us; the launch traced here: 58.8 us
  Pallas kernels  57.4 us (97%)
  local copies, waits for them, and re-layouts  1.3 us (2%)
    pallas_call x1, Pallas kernels, layer(): pl.pallas_call(functools.partial(layer_kernel, model), out_shape=jax.Shap...  48.3 us
    pallas_call x1, Pallas kernels, attend(): pl.pallas_call(attend_kernel, out_shape=jax.ShapeDtypeStruct((requests, h...  9.13 us
    unnamed x1, local copies, waits for them, and re-layouts  1.3 us

profile of v2, /device:TPU:1, one launch (start us, length us, event | category | flops | bytes accessed | tf_op | source)
XLA Modules:
  0.0 58.8 jit_solution(3545517768057393697)
XLA Ops:
  0.0 9.1 %attend.1.values = bf16[8,1024]{1,0:T(8,128)(2,1)} custom-call(s32[8]{0:T(128)} %lengths_in.1, bf16[8,1536]{1,0:T(8,128)(2,1)} %query_in.1, bf16[8,576,2048]{2,1,0:T(8,128)(2,1)} %bitcast.4, bf16[8,128,512]{2,1,0:T(8,128)(2,1)} %w_uk.1, bf16[8,512,128]{2,1,0:T(8,128)(2,1)} %w_value.1), custom_call_target="tpu_custom_call" | custom-call | tf_op jit(solution)/shard_map/attend/pallas_call | solution.py:141
  9.1 48.3 %layer.1 = bf16[8,448]{1,0:T(8,128)(2,1)} custom-call(bf16[8,1024]{1,0:T(8,128)(2,1)} %attend.1.values, bf16[448,1024]{1,0:T(8,128)(2,1)} %bitcast.6, bf16[448,128]{1,0:T(8,128)(2,1)} %bitcast.7, bf16[448]{0:T(512)(128)(2,1)} %gain_in.1, bf16[448,1152]{1,0:T(8,128)(2,1)} %w_gate.1, bf16[448,1152]{1,0:T(8,128)(2,1)} %w_up.1, bf16[448,1152]{1,0:T(8,128)(2,1)} %bitcast.5), custom_call_target="tpu_custom_call" | custom-call | tf_op jit(solution)/shard_map/layer/pallas_call | solution.py:367
  57.5 1.3 %copy.13 = bf16[8,448]{1,0:T(8,128)(2,1)} copy(bf16[8,448]{1,0:T(8,128)(2,1)} %layer.1) | data formatting | bytes 14336

commit v3 on v2

--- a/solution.py
+++ b/solution.py
@@ -21,150 +21,133 @@
 ROPE = 64
 KVR = 512
 VD = 128
-CHUNK = 512
+FIRST = 512
 VMEM_BYTES = 60 * 2**20
 NT = (((1,), (1,)), ((), ()))
 
 
-def attend_kernel(
+def project(query, w_uk, queries):
+    width = NOPE + ROPE
+    for h in range(w_uk.shape[0]):
+        nope = query[:, h * width : h * width + NOPE]
+        queries[:, h, :KVR] = jnp.dot(nope, w_uk[h], preferred_element_type=jnp.float32)
+        queries[:, h, KVR:] = query[:, h * width + NOPE : (h + 1) * width].astype(jnp.float32)
+
+
+def live_scores(query, keys, first, length):
+    got = jnp.dot(query.astype(jnp.bfloat16), keys, preferred_element_type=jnp.float32)
+    at = first + lax.broadcasted_iota(jnp.int32, got.shape, 1)
+    return jnp.where(at < length, got * (1.0 / jnp.sqrt(jnp.float32(NOPE + ROPE))), -jnp.inf)
+
+
+def weighted(probs, keys):
+    return lax.dot_general(
+        probs.astype(jnp.bfloat16), keys, NT, preferred_element_type=jnp.float32
+    )
+
+
+def later_kernel(
+    lengths_in,
+    query_in,
+    cache,
+    w_uk,
+    sums,
+    stats,
+    lengths,
+    query,
+    held,
+    uk_held,
+    queries,
+    cache_sem,
+    load_sem,
+):
+    requests = queries.shape[0]
+    most = cache.shape[2] // FIRST - 1
+    loads = [
+        pltpu.make_async_copy(src, dst, load_sem.at[at])
+        for at, (src, dst) in enumerate(
+            [(lengths_in, lengths), (w_uk, uk_held), (query_in, query)]
+        )
+    ]
+    for load in loads:
+        load.start()
+    sums[...] = jnp.zeros_like(sums)
+    stats[0] = jnp.full(stats.shape[1:], -1e30, jnp.float32)
+    stats[1] = jnp.zeros(stats.shape[1:], jnp.float32)
+    loads[0].wait()
+
+    def each(step):
+        @pl.loop(0, requests)
+        def _(b):
+            chunks = lax.div(lengths[b] - 1, FIRST)
+            for k in range(1, most + 1):
+                pl.when(chunks == k)(lambda k=k: step(b, k * FIRST))
+
+    def copy(b, width):
+        return pltpu.make_async_copy(
+            cache.at[b, :, FIRST : FIRST + width], held.at[b, :, :width], cache_sem.at[b]
+        )
+
+    each(lambda b, width: copy(b, width).start())
+    loads[1].wait()
+    loads[2].wait()
+    longest = lengths[0]
+    for b in range(1, requests):
+        longest = jnp.maximum(longest, lengths[b])
+
+    @pl.when(longest > FIRST)
+    def _():
+        project(query, uk_held, queries)
+
+        def step(b, width):
+            copy(b, width).wait()
+            scores = live_scores(queries[b], held[b, :, :width], FIRST, lengths[b])
+            top = jnp.max(scores, axis=1, keepdims=True)
+            probs = jnp.exp(scores - top)
+            total = jnp.sum(probs, axis=1, keepdims=True)
+            sums[b] = weighted(probs, held[b, :KVR, :width])
+            stats[0, b] = jnp.broadcast_to(top, stats.shape[2:])
+            stats[1, b] = jnp.broadcast_to(total, stats.shape[2:])
+
+        each(step)
+
+
+def attend_later(query, cache, lengths, w_uk):
+    requests, depth, slots = cache.shape
+    heads = w_uk.shape[0]
+    vmem = pl.BlockSpec(memory_space=pltpu.VMEM)
+    anywhere = pl.BlockSpec(memory_space=pl.ANY)
+    return pl.pallas_call(
+        later_kernel,
+        out_shape=[
+            jax.ShapeDtypeStruct((requests, heads, KVR), jnp.float32),
+            jax.ShapeDtypeStruct((2, requests, heads, 128), jnp.float32),
+        ],
+        in_specs=[anywhere] * 4,
+        out_specs=[vmem] * 2,
+        scratch_shapes=[
+            pltpu.SMEM(lengths.shape, jnp.int32),
+            pltpu.VMEM(query.shape, jnp.bfloat16),
+            pltpu.VMEM((requests, depth, slots - FIRST), jnp.bfloat16),
+            pltpu.VMEM(w_uk.shape, jnp.bfloat16),
+            pltpu.VMEM((requests, heads, depth), jnp.float32),
+            pltpu.SemaphoreType.DMA((requests,)),
+            pltpu.SemaphoreType.DMA((3,)),
+        ],
+        compiler_params=pltpu.CompilerParams(vmem_limit_bytes=VMEM_BYTES),
+        name="attend_later",
+    )(lengths, query, cache, w_uk)
+
+
+def layer_kernel(
+    model,
     lengths_in,
     query_in,
     cache,
     w_uk,
     w_value,
-    values,
-    lengths,
-    query,
-    held,
-    uk_held,
-    value_held,
-    queries,
-    scores,
-    top,
-    total,
-    context,
-    cache_sem,
-    weight_sem,
-):
-    requests, heads = queries.shape[0], queries.shape[1]
-    uk_copy = pltpu.make_async_copy(w_uk, uk_held, weight_sem.at[0])
-    value_copy = pltpu.make_async_copy(w_value, value_held, weight_sem.at[1])
-    lengths_copy = pltpu.make_async_copy(lengths_in, lengths, weight_sem.at[2])
-    query_copy = pltpu.make_async_copy(query_in, query, weight_sem.at[3])
-    lengths_copy.start()
-    query_copy.start()
-    uk_copy.start()
-
-    def chunk_copy(b, c):
-        slots = pl.ds(pl.multiple_of(c * CHUNK, CHUNK), CHUNK)
-        return pltpu.make_async_copy(
-            cache.at[b, :, slots], held.at[b, :, slots], cache_sem.at[b, c]
-        )
-
-    for b in range(requests):
-        chunk_copy(b, 0).start()
-    lengths_copy.wait()
-    chunks = [lax.div(lengths[b] + (CHUNK - 1), CHUNK) for b in range(requests)]
-    for b in range(requests):
-        pl.loop(1, chunks[b])(lambda c, b=b: chunk_copy(b, c).start())
-    value_copy.start()
-
-    query_copy.wait()
-    uk_copy.wait()
-    width = NOPE + ROPE
-    for h in range(heads):
-        nope = query[:, h * width : h * width + NOPE]
-        queries[:, h, :KVR] = jnp.dot(nope, uk_held[h], preferred_element_type=jnp.float32)
-        queries[:, h, KVR:] = query[:, h * width + NOPE : (h + 1) * width].astype(jnp.float32)
-
-    scale = 1.0 / jnp.sqrt(jnp.float32(NOPE + ROPE))
-
-    def chunk_scores(b, c):
-        slots = pl.ds(pl.multiple_of(c * CHUNK, CHUNK), CHUNK)
-        got = jnp.dot(
-            queries[b].astype(jnp.bfloat16),
-            held[b, :, slots],
-            preferred_element_type=jnp.float32,
-        )
-        at = c * CHUNK + lax.broadcasted_iota(jnp.int32, got.shape, 1)
-        got = jnp.where(at < lengths[b], got * scale, -jnp.inf)
-        scores[b, :, slots] = got
-        return jnp.max(got, axis=1, keepdims=True)
-
-    for b in range(requests):
-        chunk_copy(b, 0).wait()
-        top[b] = jnp.broadcast_to(chunk_scores(b, 0), top.shape[1:])
-    for b in range(requests):
-
-        @pl.loop(1, chunks[b])
-        def _(c, b=b):
-            chunk_copy(b, c).wait()
-            top[b] = jnp.maximum(top[b], chunk_scores(b, c))
-
-    def chunk_context(b, c):
-        slots = pl.ds(pl.multiple_of(c * CHUNK, CHUNK), CHUNK)
-        probs = jnp.exp(scores[b, :, slots] - top[b, :, :1])
-        part = lax.dot_general(
-            probs.astype(jnp.bfloat16),
-            held[b, :KVR, slots],
-            NT,
-            preferred_element_type=jnp.float32,
-        )
-        return part, jnp.sum(probs, axis=1, keepdims=True)
-
-    for b in range(requests):
-        part, sums = chunk_context(b, 0)
-        context[:, b, :] = part
-        total[b] = jnp.broadcast_to(sums, total.shape[1:])
-    for b in range(requests):
-
-        @pl.loop(1, chunks[b])
-        def _(c, b=b):
-            part, sums = chunk_context(b, c)
-            context[:, b, :] += part
-            total[b] += sums
-
-    for b in range(requests):
-        context[:, b, :] = context[:, b, :] / total[b, :, :1]
-    value_copy.wait()
-    for h in range(heads):
-        values[:, h * VD : (h + 1) * VD] = jnp.dot(
-            context[h].astype(jnp.bfloat16), value_held[h], preferred_element_type=jnp.float32
-        ).astype(jnp.bfloat16)
-
-
-def attend(query, cache, lengths, w_uk, w_value):
-    requests, depth, slots = cache.shape
-    heads = w_uk.shape[0]
-    vmem = pl.BlockSpec(memory_space=pltpu.VMEM)
-    anywhere = pl.BlockSpec(memory_space=pl.ANY)
-    return pl.pallas_call(
-        attend_kernel,
-        out_shape=jax.ShapeDtypeStruct((requests, heads * VD), jnp.bfloat16),
-        in_specs=[anywhere] * 5,
-        out_specs=vmem,
-        scratch_shapes=[
-            pltpu.SMEM(lengths.shape, jnp.int32),
-            pltpu.VMEM(query.shape, jnp.bfloat16),
-            pltpu.VMEM(cache.shape, jnp.bfloat16),
-            pltpu.VMEM(w_uk.shape, jnp.bfloat16),
-            pltpu.VMEM(w_value.shape, jnp.bfloat16),
-            pltpu.VMEM((requests, heads, depth), jnp.float32),
-            pltpu.VMEM((requests, heads, slots), jnp.float32),
-            pltpu.VMEM((requests, heads, 128), jnp.float32),
-            pltpu.VMEM((requests, heads, 128), jnp.float32),
-            pltpu.VMEM((heads, requests, KVR), jnp.float32),
-            pltpu.SemaphoreType.DMA((requests, slots // CHUNK)),
-            pltpu.SemaphoreType.DMA((4,)),
-        ],
-        compiler_params=pltpu.CompilerParams(vmem_limit_bytes=VMEM_BYTES),
-        name="attend",
-    )(lengths, query, cache, w_uk, w_value)
-
-
-def layer_kernel(
-    model,
-    values,
+    sums_in,
+    stats_in,
     w_out,
     residual,
     gain_in,
@@ -172,6 +155,17 @@
     w_up,
     w_down,
     mixed,
+    lengths,
+    query,
+    held,
+    uk_held,
+    value_held,
+    sums,
+    stats,
+    queries,
+    scores,
+    context,
+    values,
     out_held,
     gate_held,
     up_held,
@@ -194,6 +188,8 @@
     hidden_rows,
     down_send,
     down_recv,
+    attend_sem,
+    cache_sem,
     weight_sem,
     send_sem,
     recv_sem,
@@ -204,6 +200,24 @@
     columns = mixed.shape[1]
     units = gate_held.shape[1]
 
+    requests = cache.shape[0]
+    attend_loads = [
+        pltpu.make_async_copy(src, dst, attend_sem.at[at])
+        for at, (src, dst) in enumerate(
+            [
+                (w_uk, uk_held),
+                (query_in, query),
+                (lengths_in, lengths),
+                (sums_in, sums),
+                (stats_in, stats),
+                (w_value, value_held),
+            ]
+        )
+    ]
+    cache_loads = [
+        pltpu.make_async_copy(cache.at[b, :, :FIRST], held.at[b], cache_sem.at[b])
+        for b in range(requests)
+    ]
     loads = [
         pltpu.make_async_copy(src, dst, weight_sem.at[at])
         for at, (src, dst) in enumerate(
@@ -217,7 +231,7 @@
             ]
         )
     ]
-    for load in loads:
+    for load in attend_loads[:3] + cache_loads + attend_loads[3:] + loads:
         load.start()
 
     core, y, x_hi = lax.rem(dp, 2), lax.rem(dp // 2, 4), dp // 8
@@ -236,8 +250,28 @@
             pl.semaphore_signal(
                 barrier, inc=1, device_id={axis: peer(axis, d)}, device_id_type=MESH
             )
+
+    for load in attend_loads[:3]:
+        load.wait()
+    project(query, uk_held, queries)
+    for b in range(requests):
+        cache_loads[b].wait()
+        scores[b] = live_scores(queries[b], held[b], 0, lengths[b])
+    for load in attend_loads[3:]:
+        load.wait()
+    for b in range(requests):
+        later = stats[0, b, :, :1]
+        top = jnp.maximum(jnp.max(scores[b], axis=1, keepdims=True), later)
+        share = jnp.exp(later - top)
+        probs = jnp.exp(scores[b] - top)
+        total = jnp.sum(probs, axis=1, keepdims=True) + stats[1, b, :, :1] * share
+        context[:, b, :] = (weighted(probs, held[b, :KVR, :]) + sums[b] * share) / total
+    for h in range(value_held.shape[0]):
+        values[:, h * VD : (h + 1) * VD] = jnp.dot(
+            context[h].astype(jnp.bfloat16), value_held[h], preferred_element_type=jnp.float32
+        ).astype(jnp.bfloat16)
+
     pl.semaphore_wait(barrier, len(DP_PEERS) + len(TP_PEERS))
-
     finish = []
 
     def exchange(axis, phase, peers, source, target, place):
@@ -355,8 +389,24 @@
         sent()
 
 
-def layer(values, w_out, residual, gain, w_gate, w_up, w_down, groups, model):
-    rows, depth = values.shape
+def layer(
+    lengths,
+    query,
+    cache,
+    w_uk,
+    w_value,
+    sums,
+    stats,
+    w_out,
+    residual,
+    gain,
+    w_gate,
+    w_up,
+    w_down,
+    groups,
+    model,
+):
+    rows, heads, depth = cache.shape[0], w_uk.shape[0], cache.shape[1]
     columns, units = w_down.shape
     wide = -(-columns // 128) * 128
     vmem = pl.BlockSpec(memory_space=pltpu.VMEM)
@@ -367,9 +417,20 @@
     return pl.pallas_call(
         functools.partial(layer_kernel, model),
         out_shape=jax.ShapeDtypeStruct((rows, columns), jnp.bfloat16),
-        in_specs=[vmem] + [anywhere] * 6,
+        in_specs=[anywhere] * 13,
         out_specs=vmem,
         scratch_shapes=[
+            pltpu.SMEM(lengths.shape, jnp.int32),
+            pltpu.VMEM(query.shape, jnp.bfloat16),
+            pltpu.VMEM((rows, depth, FIRST), jnp.bfloat16),
+            pltpu.VMEM(w_uk.shape, jnp.bfloat16),
+            pltpu.VMEM(w_value.shape, jnp.bfloat16),
+            pltpu.VMEM(sums.shape, jnp.float32),
+            pltpu.VMEM(stats.shape, jnp.float32),
+            pltpu.VMEM((rows, heads, depth), jnp.float32),
+            pltpu.VMEM((rows, heads, FIRST), jnp.float32),
+            pltpu.VMEM((heads, rows, KVR), jnp.float32),
+            pltpu.VMEM((rows, heads * VD), jnp.bfloat16),
             pltpu.VMEM(w_out.shape, jnp.bfloat16),
             pltpu.VMEM(w_gate.shape, jnp.bfloat16),
             pltpu.VMEM(w_up.shape, jnp.bfloat16),
@@ -377,7 +438,7 @@
             pltpu.VMEM(residual.shape, jnp.bfloat16),
             pltpu.VMEM(gain.shape, jnp.bfloat16),
             pltpu.VMEM(residual.shape[::-1], jnp.float32),
-            blocks(depth),
+            blocks(heads * VD),
             blocks(wide),
             blocks(wide),
             blocks(wide),
@@ -393,6 +454,8 @@
             blocks(wide),
             blocks(wide),
             pltpu.SemaphoreType.DMA((6,)),
+            pltpu.SemaphoreType.DMA((rows,)),
+            pltpu.SemaphoreType.DMA((6,)),
             pltpu.SemaphoreType.DMA((9,)),
             pltpu.SemaphoreType.DMA((9,)),
         ],
@@ -400,7 +463,21 @@
             collective_id=0, has_side_effects=True, vmem_limit_bytes=VMEM_BYTES
         ),
         name="layer",
-    )(values, w_out, residual, gain, w_gate, w_up, w_down)
+    )(
+        lengths,
+        query,
+        cache,
+        w_uk,
+        w_value,
+        sums,
+        stats,
+        w_out,
+        residual,
+        gain,
+        w_gate,
+        w_up,
+        w_down,
+    )
 
 
 def solution(mesh):
@@ -419,9 +496,16 @@
         w_up,
         w_down,
     ):
-        values = attend(query, jnp.swapaxes(latent_cache, 1, 2), lengths, w_uk, value_up_weight)
+        cache = jnp.swapaxes(latent_cache, 1, 2)
+        sums, stats = attend_later(query, cache, lengths, w_uk)
         return layer(
-            values,
+            lengths,
+            query,
+            cache,
+            w_uk,
+            value_up_weight,
+            sums,
+            stats,
             w_out.T,
             residual.T,
             mlp_norm_scale,

time: 59 us -> 55.5 us (0.941)
  Pallas kernels: 57.4 us -> 54 us
    pallas_call x1, Pallas kernels: 9.13 us -> 2 us  [attend_later(): pl.pallas_call(later_kernel, out_shape=[jax.ShapeDtypeStruct((requests, h...]
    pallas_call x1, Pallas kernels: 48.3 us -> 52 us  [layer(): pl.pallas_call(functools.partial(layer_kernel, model), out_shape=jax.Shap...]
where the time goes in v3:
time: 55.5 us; the launch traced here: 55.3 us
  Pallas kernels  54 us (97%)
  local copies, waits for them, and re-layouts  1.3 us (2%)
    pallas_call x1, Pallas kernels, layer(): pl.pallas_call(functools.partial(layer_kernel, model), out_shape=jax.Shap...  52 us
    pallas_call x1, Pallas kernels, attend_later(): pl.pallas_call(later_kernel, out_shape=[jax.ShapeDtypeStruct((requests, h...  2 us
    unnamed x1, local copies, waits for them, and re-layouts  1.3 us

profile of v3, /device:TPU:1, one launch (start us, length us, event | category | flops | bytes accessed | tf_op | source)
XLA Modules:
  0.0 55.3 jit_solution(476813996482553389)
XLA Ops:
  0.0 2.0 %attend_later.1 = (f32[8,8,512]{2,1,0:T(8,128)}, f32[2,8,8,128]{3,2,1,0:T(8,128)}) custom-call(s32[8]{0:T(128)} %lengths_in.3, bf16[8,1536]{1,0:T(8,128)(2,1)} %query_in.3, bf16[8,576,2048]{2,1,0:T(8,128)(2,1)} %bitcast.4, bf16[8,128,512]{2,1,0:T(8,128)(2,1)} %w_uk.3), custom_call_target="tpu_custom_call" | custom-call | tf_op jit(solution)/shard_map/attend_later/pallas_call | solution.py:120
  2.0 52.0 %layer.1 = bf16[8,448]{1,0:T(8,128)(2,1)} custom-call(s32[8]{0:T(128)} %lengths_in.3, bf16[8,1536]{1,0:T(8,128)(2,1)} %query_in.3, bf16[8,576,2048]{2,1,0:T(8,128)(2,1)} %bitcast.5, bf16[8,128,512]{2,1,0:T(8,128)(2,1)} %w_uk.3, bf16[8,512,128]{2,1,0:T(8,128)(2,1)} %w_value.1, f32[8,8,512]{2,1,0:T(8,128)} %get-tuple-element.7.sums_in, ...), custom_call_target="tpu_custom_call" | custom-call | tf_op jit(solution)/shard_map/layer/pallas_call | solution.py:417
  54.0 1.3 %copy.13 = bf16[8,448]{1,0:T(8,128)(2,1)} copy(bf16[8,448]{1,0:T(8,128)(2,1)} %layer.1) | data formatting | bytes 14336

commit v4 on v3

--- a/solution.py
+++ b/solution.py
@@ -7,11 +7,11 @@
 from jax.experimental.pallas import tpu as pltpu
 from jax.sharding import PartitionSpec as P
 
-DP_PEERS = sorted(
-    [(a, b, c) for a in range(2) for b in range(4) for c in range(2) if a + b + c],
+CHIP_PEERS = sorted(
+    [(a, b, 0) for a in range(2) for b in range(4) if a + b],
     key=lambda d: -(2 * d[0] + min(d[1], 4 - d[1])),
 )
-CHIP_PEERS = [d for d in DP_PEERS if d[2] == 0]
+DP_PEERS = CHIP_PEERS + [(0, 0, 1)]
 TP_PEERS = sorted(
     [(a, b) for a in range(8) for b in range(2) if a + b],
     key=lambda d: -(min(d[0], 8 - d[0]) + d[1]),
@@ -35,7 +35,7 @@
 
 
 def live_scores(query, keys, first, length):
-    got = jnp.dot(query.astype(jnp.bfloat16), keys, preferred_element_type=jnp.float32)
+    got = jnp.dot(query, keys, preferred_element_type=jnp.float32)
     at = first + lax.broadcasted_iota(jnp.int32, got.shape, 1)
     return jnp.where(at < length, got * (1.0 / jnp.sqrt(jnp.float32(NOPE + ROPE))), -jnp.inf)
 
@@ -51,13 +51,14 @@
     query_in,
     cache,
     w_uk,
+    queries,
     sums,
     stats,
     lengths,
     query,
     held,
     uk_held,
-    queries,
+    wide_queries,
     cache_sem,
     load_sem,
 ):
@@ -91,14 +92,14 @@
     each(lambda b, width: copy(b, width).start())
     loads[1].wait()
     loads[2].wait()
+    project(query, uk_held, wide_queries)
+    queries[...] = wide_queries[...].astype(jnp.bfloat16)
     longest = lengths[0]
     for b in range(1, requests):
         longest = jnp.maximum(longest, lengths[b])
 
     @pl.when(longest > FIRST)
     def _():
-        project(query, uk_held, queries)
-
         def step(b, width):
             copy(b, width).wait()
             scores = live_scores(queries[b], held[b, :, :width], FIRST, lengths[b])
@@ -120,11 +121,12 @@
     return pl.pallas_call(
         later_kernel,
         out_shape=[
+            jax.ShapeDtypeStruct((requests, heads, depth), jnp.bfloat16),
             jax.ShapeDtypeStruct((requests, heads, KVR), jnp.float32),
             jax.ShapeDtypeStruct((2, requests, heads, 128), jnp.float32),
         ],
         in_specs=[anywhere] * 4,
-        out_specs=[vmem] * 2,
+        out_specs=[vmem] * 3,
         scratch_shapes=[
             pltpu.SMEM(lengths.shape, jnp.int32),
             pltpu.VMEM(query.shape, jnp.bfloat16),
@@ -142,10 +144,9 @@
 def layer_kernel(
     model,
     lengths_in,
-    query_in,
     cache,
-    w_uk,
     w_value,
+    queries_in,
     sums_in,
     stats_in,
     w_out,
@@ -156,14 +157,11 @@
     w_down,
     mixed,
     lengths,
-    query,
     held,
-    uk_held,
     value_held,
+    queries,
     sums,
     stats,
-    queries,
-    scores,
     context,
     values,
     out_held,
@@ -185,6 +183,7 @@
     up_other,
     up_send,
     up_recv,
+    hidden_block,
     hidden_rows,
     down_send,
     down_recv,
@@ -195,7 +194,7 @@
     recv_sem,
 ):
     dp, tp = lax.axis_index("dp"), lax.axis_index("tp")
-    groups = all_values.shape[0]
+    groups = 2 * all_values.shape[1]
     rows = values.shape[0]
     columns = mixed.shape[1]
     units = gate_held.shape[1]
@@ -205,11 +204,10 @@
         pltpu.make_async_copy(src, dst, attend_sem.at[at])
         for at, (src, dst) in enumerate(
             [
-                (w_uk, uk_held),
-                (query_in, query),
+                (queries_in, queries),
                 (lengths_in, lengths),
+                (stats_in, stats),
                 (sums_in, sums),
-                (stats_in, stats),
                 (w_value, value_held),
             ]
         )
@@ -231,9 +229,10 @@
             ]
         )
     ]
-    for load in attend_loads[:3] + cache_loads + attend_loads[3:] + loads:
+    for load in attend_loads[:4] + cache_loads + attend_loads[4:] + loads:
         load.start()
 
+    chip = dp // 2
     core, y, x_hi = lax.rem(dp, 2), lax.rem(dp // 2, 4), dp // 8
     x_lo, z = lax.rem(tp, 2), tp // 2
 
@@ -251,21 +250,26 @@
                 barrier, inc=1, device_id={axis: peer(axis, d)}, device_id_type=MESH
             )
 
-    for load in attend_loads[:3]:
+    for load in attend_loads[:4]:
         load.wait()
-    project(query, uk_held, queries)
+
+    def finish_request(b, scores):
+        later = stats[0, b, :, :1]
+        top = jnp.maximum(jnp.max(scores, axis=1, keepdims=True), later)
+        share = jnp.exp(later - top)
+        probs = jnp.exp(scores - top)
+        total = jnp.sum(probs, axis=1, keepdims=True) + stats[1, b, :, :1] * share
+        context[:, b, :] = (weighted(probs, held[b, :KVR, :]) + sums[b] * share) / total
+
+    before = None
     for b in range(requests):
         cache_loads[b].wait()
-        scores[b] = live_scores(queries[b], held[b], 0, lengths[b])
-    for load in attend_loads[3:]:
-        load.wait()
-    for b in range(requests):
-        later = stats[0, b, :, :1]
-        top = jnp.maximum(jnp.max(scores[b], axis=1, keepdims=True), later)
-        share = jnp.exp(later - top)
-        probs = jnp.exp(scores[b] - top)
-        total = jnp.sum(probs, axis=1, keepdims=True) + stats[1, b, :, :1] * share
-        context[:, b, :] = (weighted(probs, held[b, :KVR, :]) + sums[b] * share) / total
+        scores = live_scores(queries[b], held[b], 0, lengths[b])
+        if b:
+            finish_request(b - 1, before)
+        before = scores
+    finish_request(requests - 1, before)
+    attend_loads[4].wait()
     for h in range(value_held.shape[0]):
         values[:, h * VD : (h + 1) * VD] = jnp.dot(
             context[h].astype(jnp.bfloat16), value_held[h], preferred_element_type=jnp.float32
@@ -273,6 +277,11 @@
 
     pl.semaphore_wait(barrier, len(DP_PEERS) + len(TP_PEERS))
     finish = []
+
+    def by_chip(blocks, wide):
+        wide = wide.astype(jnp.bfloat16).reshape(2, groups // 2, rows, columns)
+        blocks[:, 0, :, :columns] = wide[0]
+        blocks[:, 1, :, :columns] = wide[1]
 
     def exchange(axis, phase, peers, source, target, place):
         for d in peers:
@@ -289,8 +298,30 @@
         finish.append(pltpu.make_async_copy(blocks, blocks, send_sem.at[phase]).wait)
         return pltpu.make_async_copy(blocks, blocks, recv_sem.at[phase]).wait
 
-    arrive = exchange("dp", 0, DP_PEERS, lambda to: values, all_values, dp)
-    all_values[dp] = values[...]
+    other_core = {"dp": peer("dp", (0, 0, 1))}
+
+    def gather(phase, block, target):
+        arrive = exchange("dp", phase, CHIP_PEERS, lambda to: block, target.at[core], chip)
+        target[core, chip] = block[...]
+
+        def finished():
+            arrive()
+            copy = pltpu.make_async_remote_copy(
+                src_ref=target.at[core],
+                dst_ref=target.at[core],
+                send_sem=send_sem.at[phase + 9],
+                recv_sem=recv_sem.at[phase + 9],
+                device_id=other_core,
+                device_id_type=MESH,
+            )
+            copy.start()
+            finish.append(copy.wait_send)
+            theirs = target.at[1 - core]
+            pltpu.make_async_copy(theirs, theirs, recv_sem.at[phase + 9]).wait()
+
+        return finished
+
+    arrive = gather(0, values, all_values)
     loads[1].wait()
     residual_rows[...] = residual_held[...].astype(jnp.float32).T
     loads[0].wait()
@@ -301,17 +332,19 @@
         NT,
         preferred_element_type=jnp.float32,
     )
-    out_send[:, :, :columns] = attended.astype(jnp.bfloat16).reshape(groups, rows, columns)
-
-    arrive = exchange("tp", 1, TP_PEERS, lambda to: out_send.at[to], out_recv, tp)
-    out_recv[tp] = out_send[tp]
+    by_chip(out_send, attended)
+
+    arrive = exchange(
+        "tp", 2, TP_PEERS, lambda to: out_send.at[to // 2, lax.rem(to, 2)], out_recv, tp
+    )
+    out_recv[tp] = out_send[tp // 2, x_lo]
     arrive()
     own = residual_rows[pl.ds(pl.multiple_of(tp * rows, rows), rows), :]
     own = own + jnp.sum(out_recv[:, :, :columns].astype(jnp.float32), axis=0)
     own = own.astype(jnp.bfloat16)
     stream_rows[tp, :, :columns] = own
 
-    arrive = exchange("tp", 2, TP_PEERS, lambda to: stream_rows.at[tp], stream_rows, tp)
+    arrive = exchange("tp", 3, TP_PEERS, lambda to: stream_rows.at[tp], stream_rows, tp)
     loads[2].wait()
     loads[3].wait()
     loads[4].wait()
@@ -333,7 +366,7 @@
             dst_ref=pair_recv,
             send_sem=send_sem.at[5 + part],
             recv_sem=recv_sem.at[5 + part],
-            device_id={"dp": peer("dp", (0, 0, 1))},
+            device_id=other_core,
             device_id_type=MESH,
         )
         copy.start()
@@ -351,9 +384,9 @@
         both = pair_send[core].astype(jnp.float32) + pair_recv[...].astype(jnp.float32)
         send[...] = both.astype(jnp.bfloat16)
         arrive = exchange(
-            "dp", 7 + part, CHIP_PEERS, lambda to: send.at[to // 2], recv, dp // 2
-        )
-        recv[dp // 2] = send[dp // 2]
+            "dp", 7 + part, CHIP_PEERS, lambda to: send.at[to // 2], recv, chip
+        )
+        recv[chip] = send[chip]
         return arrive
 
     gate_arrive = scatter(0, gate_copy, gate_pair, gate_other, gate_send, gate_recv)
@@ -367,9 +400,9 @@
     gate = gate * inv_rms
     up = up[:, :units] * inv_rms
     hidden = gate / (1.0 + jnp.exp(-gate)) * up
-    hidden_rows[dp] = hidden.astype(jnp.bfloat16)
-
-    arrive = exchange("dp", 3, DP_PEERS, lambda to: hidden_rows.at[dp], hidden_rows, dp)
+    hidden_block[...] = hidden.astype(jnp.bfloat16)
+
+    arrive = gather(1, hidden_block, hidden_rows)
     loads[5].wait()
     arrive()
     down = lax.dot_general(
@@ -378,10 +411,12 @@
         NT,
         preferred_element_type=jnp.float32,
     )
-    down_send[:, :, :columns] = down.astype(jnp.bfloat16).reshape(groups, rows, columns)
-
-    arrive = exchange("tp", 4, TP_PEERS, lambda to: down_send.at[to], down_recv, tp)
-    down_recv[tp] = down_send[tp]
+    by_chip(down_send, down)
+
+    arrive = exchange(
+        "tp", 4, TP_PEERS, lambda to: down_send.at[to // 2, lax.rem(to, 2)], down_recv, tp
+    )
+    down_recv[tp] = down_send[tp // 2, x_lo]
     arrive()
     result = jnp.sum(down_recv[:, :, :columns].astype(jnp.float32), axis=0)
     mixed[...] = (own.astype(jnp.float32) + result).astype(jnp.bfloat16)
@@ -391,10 +426,9 @@
 
 def layer(
     lengths,
-    query,
     cache,
-    w_uk,
     w_value,
+    queries,
     sums,
     stats,
     w_out,
@@ -406,29 +440,27 @@
     groups,
     model,
 ):
-    rows, heads, depth = cache.shape[0], w_uk.shape[0], cache.shape[1]
+    rows, heads, depth = queries.shape
     columns, units = w_down.shape
     wide = -(-columns // 128) * 128
     vmem = pl.BlockSpec(memory_space=pltpu.VMEM)
     anywhere = pl.BlockSpec(memory_space=pl.ANY)
     blocks = lambda width: pltpu.VMEM((groups, rows, width), jnp.bfloat16)
+    chips = lambda width: pltpu.VMEM((groups // 2, 2, rows, width), jnp.bfloat16)
     half = lambda width: pltpu.VMEM((groups // 2, rows, width), jnp.bfloat16)
     pair = lambda width: pltpu.VMEM((2, groups // 2, rows, width), jnp.bfloat16)
     return pl.pallas_call(
         functools.partial(layer_kernel, model),
         out_shape=jax.ShapeDtypeStruct((rows, columns), jnp.bfloat16),
-        in_specs=[anywhere] * 13,
+        in_specs=[anywhere] * 12,
         out_specs=vmem,
         scratch_shapes=[
             pltpu.SMEM(lengths.shape, jnp.int32),
-            pltpu.VMEM(query.shape, jnp.bfloat16),
             pltpu.VMEM((rows, depth, FIRST), jnp.bfloat16),
-            pltpu.VMEM(w_uk.shape, jnp.bfloat16),
             pltpu.VMEM(w_value.shape, jnp.bfloat16),
+            pltpu.VMEM(queries.shape, jnp.bfloat16),
             pltpu.VMEM(sums.shape, jnp.float32),
             pltpu.VMEM(stats.shape, jnp.float32),
-            pltpu.VMEM((rows, heads, depth), jnp.float32),
-            pltpu.VMEM((rows, heads, FIRST), jnp.float32),
             pltpu.VMEM((heads, rows, KVR), jnp.float32),
             pltpu.VMEM((rows, heads * VD), jnp.bfloat16),
             pltpu.VMEM(w_out.shape, jnp.bfloat16),
@@ -438,8 +470,8 @@
             pltpu.VMEM(residual.shape, jnp.bfloat16),
             pltpu.VMEM(gain.shape, jnp.bfloat16),
             pltpu.VMEM(residual.shape[::-1], jnp.float32),
-            blocks(heads * VD),
-            blocks(wide),
+            pair(heads * VD),
+            chips(wide),
             blocks(wide),
             blocks(wide),
             pair(units),
@@ -450,14 +482,15 @@
             half(units + 128),
             half(units + 128),
             half(units + 128),
-            blocks(units),
+            pltpu.VMEM((rows, units), jnp.bfloat16),
+            pair(units),
+            chips(wide),
             blocks(wide),
-            blocks(wide),
-            pltpu.SemaphoreType.DMA((6,)),
+            pltpu.SemaphoreType.DMA((5,)),
             pltpu.SemaphoreType.DMA((rows,)),
             pltpu.SemaphoreType.DMA((6,)),
-            pltpu.SemaphoreType.DMA((9,)),
-            pltpu.SemaphoreType.DMA((9,)),
+            pltpu.SemaphoreType.DMA((11,)),
+            pltpu.SemaphoreType.DMA((11,)),
         ],
         compiler_params=pltpu.CompilerParams(
             collective_id=0, has_side_effects=True, vmem_limit_bytes=VMEM_BYTES
@@ -465,10 +498,9 @@
         name="layer",
     )(
         lengths,
-        query,
         cache,
-        w_uk,
         w_value,
+        queries,
         sums,
         stats,
         w_out,
@@ -497,13 +529,12 @@
         w_down,
     ):
         cache = jnp.swapaxes(latent_cache, 1, 2)
-        sums, stats = attend_later(query, cache, lengths, w_uk)
+        queries, sums, stats = attend_later(query, cache, lengths, w_uk)
         return layer(
             lengths,
-            query,
             cache,
-            w_uk,
             value_up_weight,
+            queries,
             sums,
             stats,
             w_out.T,

time: 55.5 us -> 57.3 us (1.032)
  Pallas kernels: 54 us -> 55.8 us
    pallas_call x1, Pallas kernels: 52 us -> 53.5 us  [layer(): pl.pallas_call(functools.partial(layer_kernel, model), out_shape=jax.Shap...]
where the time goes in v4:
time: 57.3 us; the launch traced here: 57.1 us
  Pallas kernels  55.8 us (97%)
  local copies, waits for them, and re-layouts  1.3 us (2%)
    pallas_call x1, Pallas kernels, layer(): pl.pallas_call(functools.partial(layer_kernel, model), out_shape=jax.Shap...  53.5 us
    pallas_call x1, Pallas kernels, attend_later(): pl.pallas_call(later_kernel, out_shape=[jax.ShapeDtypeStruct((requests, h...  2.34 us
    unnamed x1, local copies, waits for them, and re-layouts  1.3 us

profile of v4, /device:TPU:1, one launch (start us, length us, event | category | flops | bytes accessed | tf_op | source)
XLA Modules:
  0.0 57.1 jit_solution(13462153293749243791)
XLA Ops:
  0.0 2.3 %attend_later.1 = (bf16[8,8,576]{2,1,0:T(8,128)(2,1)}, f32[8,8,512]{2,1,0:T(8,128)}, f32[2,8,8,128]{3,2,1,0:T(8,128)}) custom-call(s32[8]{0:T(128)} %lengths_in.3, bf16[8,1536]{1,0:T(8,128)(2,1)} %query_in.1, bf16[8,576,2048]{2,1,0:T(8,128)(2,1)} %bitcast.4, bf16[8,128,512]{2,1,0:T(8,128)(2,1)} %w_uk.1), custom_call_target="tpu_custom_call" | custom-call | tf_op jit(solution)/shard_map/attend_later/pallas_call | solution.py:121
  2.3 53.5 %layer.1 = bf16[8,448]{1,0:T(8,128)(2,1)} custom-call(s32[8]{0:T(128)} %lengths_in.3, bf16[8,576,2048]{2,1,0:T(8,128)(2,1)} %bitcast.5, bf16[8,512,128]{2,1,0:T(8,128)(2,1)} %w_value.1, bf16[8,8,576]{2,1,0:T(8,128)(2,1)} %get-tuple-element.8.queries_in, f32[8,8,512]{2,1,0:T(8,128)} %get-tuple-element.9.sums_in, f32[2,8,8,128]{3,2,1,0:T(8,128)} %get-tuple-element.10.stats_in, ...), custom_call_target="tpu_custom_call" | custom-call | tf_op jit(solution)/shard_map/layer/pallas_call | solution.py:452
  55.8 1.3 %copy.13 = bf16[8,448]{1,0:T(8,128)(2,1)} copy(bf16[8,448]{1,0:T(8,128)(2,1)} %layer.1) | data formatting | bytes 14336

commit v5 on v4

--- a/solution.py
+++ b/solution.py
@@ -7,11 +7,11 @@
 from jax.experimental.pallas import tpu as pltpu
 from jax.sharding import PartitionSpec as P
 
-CHIP_PEERS = sorted(
-    [(a, b, 0) for a in range(2) for b in range(4) if a + b],
+DP_PEERS = sorted(
+    [(a, b, c) for a in range(2) for b in range(4) for c in range(2) if a + b + c],
     key=lambda d: -(2 * d[0] + min(d[1], 4 - d[1])),
 )
-DP_PEERS = CHIP_PEERS + [(0, 0, 1)]
+CHIP_PEERS = [d for d in DP_PEERS if d[2] == 0]
 TP_PEERS = sorted(
     [(a, b) for a in range(8) for b in range(2) if a + b],
     key=lambda d: -(min(d[0], 8 - d[0]) + d[1]),
@@ -22,6 +22,7 @@
 KVR = 512
 VD = 128
 FIRST = 512
+TOGETHER = 4
 VMEM_BYTES = 60 * 2**20
 NT = (((1,), (1,)), ((), ()))
 
@@ -194,7 +195,7 @@
     recv_sem,
 ):
     dp, tp = lax.axis_index("dp"), lax.axis_index("tp")
-    groups = 2 * all_values.shape[1]
+    groups = all_values.shape[0]
     rows = values.shape[0]
     columns = mixed.shape[1]
     units = gate_held.shape[1]
@@ -259,16 +260,19 @@
         share = jnp.exp(later - top)
         probs = jnp.exp(scores - top)
         total = jnp.sum(probs, axis=1, keepdims=True) + stats[1, b, :, :1] * share
-        context[:, b, :] = (weighted(probs, held[b, :KVR, :]) + sums[b] * share) / total
-
-    before = None
-    for b in range(requests):
-        cache_loads[b].wait()
-        scores = live_scores(queries[b], held[b], 0, lengths[b])
-        if b:
-            finish_request(b - 1, before)
-        before = scores
-    finish_request(requests - 1, before)
+        context[:, b, :] = (weighted(probs, held[b, :KVR, :]) + sums[b] * share) * (1.0 / total)
+
+    before = []
+    for first in range(0, requests, TOGETHER):
+        some = range(first, first + TOGETHER)
+        for b in some:
+            cache_loads[b].wait()
+        now = [(b, live_scores(queries[b], held[b], 0, lengths[b])) for b in some]
+        for b, scores in before:
+            finish_request(b, scores)
+        before = now
+    for b, scores in before:
+        finish_request(b, scores)
     attend_loads[4].wait()
     for h in range(value_held.shape[0]):
         values[:, h * VD : (h + 1) * VD] = jnp.dot(
@@ -278,10 +282,8 @@
     pl.semaphore_wait(barrier, len(DP_PEERS) + len(TP_PEERS))
     finish = []
 
-    def by_chip(blocks, wide):
-        wide = wide.astype(jnp.bfloat16).reshape(2, groups // 2, rows, columns)
-        blocks[:, 0, :, :columns] = wide[0]
-        blocks[:, 1, :, :columns] = wide[1]
+    def in_blocks(blocks, wide):
+        blocks[:, :, :columns] = wide.astype(jnp.bfloat16).reshape(groups, rows, columns)
 
     def exchange(axis, phase, peers, source, target, place):
         for d in peers:
@@ -301,25 +303,9 @@
     other_core = {"dp": peer("dp", (0, 0, 1))}
 
     def gather(phase, block, target):
-        arrive = exchange("dp", phase, CHIP_PEERS, lambda to: block, target.at[core], chip)
-        target[core, chip] = block[...]
-
-        def finished():
-            arrive()
-            copy = pltpu.make_async_remote_copy(
-                src_ref=target.at[core],
-                dst_ref=target.at[core],
-                send_sem=send_sem.at[phase + 9],
-                recv_sem=recv_sem.at[phase + 9],
-                device_id=other_core,
-                device_id_type=MESH,
-            )
-            copy.start()
-            finish.append(copy.wait_send)
-            theirs = target.at[1 - core]
-            pltpu.make_async_copy(theirs, theirs, recv_sem.at[phase + 9]).wait()
-
-        return finished
+        arrive = exchange("dp", phase, DP_PEERS, lambda to: block, target, dp)
+        target[dp] = block[...]
+        return arrive
 
     arrive = gather(0, values, all_values)
     loads[1].wait()
@@ -332,12 +318,10 @@
         NT,
         preferred_element_type=jnp.float32,
     )
-    by_chip(out_send, attended)
-
-    arrive = exchange(
-        "tp", 2, TP_PEERS, lambda to: out_send.at[to // 2, lax.rem(to, 2)], out_recv, tp
-    )
-    out_recv[tp] = out_send[tp // 2, x_lo]
+    in_blocks(out_send, attended)
+
+    arrive = exchange("tp", 2, TP_PEERS, lambda to: out_send.at[to], out_recv, tp)
+    out_recv[tp] = out_send[tp]
     arrive()
     own = residual_rows[pl.ds(pl.multiple_of(tp * rows, rows), rows), :]
     own = own + jnp.sum(out_recv[:, :, :columns].astype(jnp.float32), axis=0)
@@ -411,12 +395,10 @@
         NT,
         preferred_element_type=jnp.float32,
     )
-    by_chip(down_send, down)
-
-    arrive = exchange(
-        "tp", 4, TP_PEERS, lambda to: down_send.at[to // 2, lax.rem(to, 2)], down_recv, tp
-    )
-    down_recv[tp] = down_send[tp // 2, x_lo]
+    in_blocks(down_send, down)
+
+    arrive = exchange("tp", 4, TP_PEERS, lambda to: down_send.at[to], down_recv, tp)
+    down_recv[tp] = down_send[tp]
     arrive()
     result = jnp.sum(down_recv[:, :, :columns].astype(jnp.float32), axis=0)
     mixed[...] = (own.astype(jnp.float32) + result).astype(jnp.bfloat16)
@@ -446,7 +428,6 @@
     vmem = pl.BlockSpec(memory_space=pltpu.VMEM)
     anywhere = pl.BlockSpec(memory_space=pl.ANY)
     blocks = lambda width: pltpu.VMEM((groups, rows, width), jnp.bfloat16)
-    chips = lambda width: pltpu.VMEM((groups // 2, 2, rows, width), jnp.bfloat16)
     half = lambda width: pltpu.VMEM((groups // 2, rows, width), jnp.bfloat16)
     pair = lambda width: pltpu.VMEM((2, groups // 2, rows, width), jnp.bfloat16)
     return pl.pallas_call(
@@ -470,8 +451,8 @@
             pltpu.VMEM(residual.shape, jnp.bfloat16),
             pltpu.VMEM(gain.shape, jnp.bfloat16),
             pltpu.VMEM(residual.shape[::-1], jnp.float32),
-            pair(heads * VD),
-            chips(wide),
+            blocks(heads * VD),
+            blocks(wide),
             blocks(wide),
             blocks(wide),
             pair(units),
@@ -483,14 +464,14 @@
             half(units + 128),
             half(units + 128),
             pltpu.VMEM((rows, units), jnp.bfloat16),
-            pair(units),
-            chips(wide),
+            blocks(units),
+            blocks(wide),
             blocks(wide),
             pltpu.SemaphoreType.DMA((5,)),
             pltpu.SemaphoreType.DMA((rows,)),
             pltpu.SemaphoreType.DMA((6,)),
-            pltpu.SemaphoreType.DMA((11,)),
-            pltpu.SemaphoreType.DMA((11,)),
+            pltpu.SemaphoreType.DMA((9,)),
+            pltpu.SemaphoreType.DMA((9,)),
         ],
         compiler_params=pltpu.CompilerParams(
             collective_id=0, has_side_effects=True, vmem_limit_bytes=VMEM_BYTES

time: 57.3 us -> 54.8 us (0.956)
  Pallas kernels: 55.8 us -> 53.3 us
    pallas_call x1, Pallas kernels: 53.5 us -> 49.4 us  [layer(): pl.pallas_call(functools.partial(layer_kernel, model), out_shape=jax.Shap...]
    pallas_call x1, Pallas kernels: 2.34 us -> 3.96 us  [attend_later(): pl.pallas_call(later_kernel, out_shape=[jax.ShapeDtypeStruct((requests, h...]
where the time goes in v5:
time: 54.8 us; the launch traced here: 54.7 us
  Pallas kernels  53.3 us (97%)
  local copies, waits for them, and re-layouts  1.3 us (2%)
    pallas_call x1, Pallas kernels, layer(): pl.pallas_call(functools.partial(layer_kernel, model), out_shape=jax.Shap...  49.4 us
    pallas_call x1, Pallas kernels, attend_later(): pl.pallas_call(later_kernel, out_shape=[jax.ShapeDtypeStruct((requests, h...  3.96 us
    unnamed x1, local copies, waits for them, and re-layouts  1.3 us

profile of v5, /device:TPU:1, one launch (start us, length us, event | category | flops | bytes accessed | tf_op | source)
XLA Modules:
  0.0 54.7 jit_solution(6890440899008565981)
XLA Ops:
  0.0 4.0 %attend_later.1 = (bf16[8,8,576]{2,1,0:T(8,128)(2,1)}, f32[8,8,512]{2,1,0:T(8,128)}, f32[2,8,8,128]{3,2,1,0:T(8,128)}) custom-call(s32[8]{0:T(128)} %lengths_in.3, bf16[8,1536]{1,0:T(8,128)(2,1)} %query_in.1, bf16[8,576,2048]{2,1,0:T(8,128)(2,1)} %bitcast.4, bf16[8,128,512]{2,1,0:T(8,128)(2,1)} %w_uk.1), custom_call_target="tpu_custom_call" | custom-call | tf_op jit(solution)/shard_map/attend_later/pallas_call | solution.py:122
  4.0 49.4 %layer.1 = bf16[8,448]{1,0:T(8,128)(2,1)} custom-call(s32[8]{0:T(128)} %lengths_in.3, bf16[8,576,2048]{2,1,0:T(8,128)(2,1)} %bitcast.5, bf16[8,512,128]{2,1,0:T(8,128)(2,1)} %w_value.1, bf16[8,8,576]{2,1,0:T(8,128)(2,1)} %get-tuple-element.8.queries_in, f32[8,8,512]{2,1,0:T(8,128)} %get-tuple-element.9.sums_in, f32[2,8,8,128]{3,2,1,0:T(8,128)} %get-tuple-element.10.stats_in, ...), custom_call_target="tpu_custom_call" | custom-call | tf_op jit(solution)/shard_map/layer/pallas_call | solution.py:433
  53.4 1.3 %copy.13 = bf16[8,448]{1,0:T(8,128)(2,1)} copy(bf16[8,448]{1,0:T(8,128)(2,1)} %layer.1) | data formatting | bytes 14336

commit v6 on v5

--- a/solution.py
+++ b/solution.py
@@ -7,11 +7,10 @@
 from jax.experimental.pallas import tpu as pltpu
 from jax.sharding import PartitionSpec as P
 
-DP_PEERS = sorted(
-    [(a, b, c) for a in range(2) for b in range(4) for c in range(2) if a + b + c],
+CHIP_PEERS = sorted(
+    [(a, b) for a in range(2) for b in range(4) if a + b],
     key=lambda d: -(2 * d[0] + min(d[1], 4 - d[1])),
 )
-CHIP_PEERS = [d for d in DP_PEERS if d[2] == 0]
 TP_PEERS = sorted(
     [(a, b) for a in range(8) for b in range(2) if a + b],
     key=lambda d: -(min(d[0], 8 - d[0]) + d[1]),
@@ -175,18 +174,20 @@
     all_values,
     out_send,
     out_recv,
+    gains,
+    stream_own,
     stream_rows,
-    gate_pair,
-    gate_other,
-    gate_send,
-    gate_recv,
-    up_pair,
-    up_other,
-    up_send,
-    up_recv,
+    base,
+    first_send,
+    first_recv,
+    second_send,
+    second_recv,
     hidden_block,
     hidden_rows,
+    rest_block,
+    rest_rows,
     down_send,
+    down_other,
     down_recv,
     attend_sem,
     cache_sem,
@@ -195,11 +196,15 @@
     recv_sem,
 ):
     dp, tp = lax.axis_index("dp"), lax.axis_index("tp")
-    groups = all_values.shape[0]
+    groups = out_recv.shape[0]
     rows = values.shape[0]
     columns = mixed.shape[1]
-    units = gate_held.shape[1]
-
+    units = gate_held.shape[2]
+    chips = groups // 2
+
+    chip = dp // 2
+    core, y, x_hi = lax.rem(dp, 2), lax.rem(dp // 2, 4), dp // 8
+    x_lo, z = lax.rem(tp, 2), tp // 2
     requests = cache.shape[0]
     attend_loads = [
         pltpu.make_async_copy(src, dst, attend_sem.at[at])
@@ -221,35 +226,30 @@
         pltpu.make_async_copy(src, dst, weight_sem.at[at])
         for at, (src, dst) in enumerate(
             [
-                (w_out, out_held),
-                (residual, residual_held),
+                (w_out, out_held.at[core]),
+                (residual, residual_held.at[core]),
                 (gain_in, gain),
-                (w_gate, gate_held),
-                (w_up, up_held),
-                (w_down, down_held),
+                (w_gate, gate_held.at[core]),
+                (w_up, up_held.at[core]),
+                (w_down, down_held.at[core]),
             ]
         )
     ]
     for load in attend_loads[:4] + cache_loads + attend_loads[4:] + loads:
         load.start()
 
-    chip = dp // 2
-    core, y, x_hi = lax.rem(dp, 2), lax.rem(dp // 2, 4), dp // 8
-    x_lo, z = lax.rem(tp, 2), tp // 2
-
-    def peer(axis, d):
+    def along(axis, d):
         if axis == "dp":
-            return (
-                lax.rem(x_hi + d[0], 2) * 8 + lax.rem(y + d[1], 4) * 2 + lax.rem(core + d[2], 2)
-            )
-        return lax.rem(z + d[0], 8) * 2 + lax.rem(x_lo + d[1], 2)
-
+            return {"dp": lax.rem(x_hi + d[0], 2) * 8 + lax.rem(y + d[1], 4) * 2 + core}
+        return {"tp": lax.rem(z + d[0], 8) * 2 + lax.rem(x_lo + d[1], 2)}
+
+    other_dp = chip * 2 + 1 - core
+    other_core = {"dp": other_dp, "tp": tp}
     barrier = pltpu.get_barrier_semaphore()
-    for axis, peers in (("dp", DP_PEERS), ("tp", TP_PEERS)):
-        for d in peers:
-            pl.semaphore_signal(
-                barrier, inc=1, device_id={axis: peer(axis, d)}, device_id_type=MESH
-            )
+    partners = [along("dp", d) for d in CHIP_PEERS] + [along("tp", d) for d in TP_PEERS]
+    partners.append(other_core)
+    for partner in partners:
+        pl.semaphore_signal(barrier, inc=1, device_id=partner, device_id_type=MESH)
 
     for load in attend_loads[:4]:
         load.wait()
@@ -279,129 +279,179 @@
             context[h].astype(jnp.bfloat16), value_held[h], preferred_element_type=jnp.float32
         ).astype(jnp.bfloat16)
 
-    pl.semaphore_wait(barrier, len(DP_PEERS) + len(TP_PEERS))
+    pl.semaphore_wait(barrier, len(partners))
     finish = []
 
-    def in_blocks(blocks, wide):
-        blocks[:, :, :columns] = wide.astype(jnp.bfloat16).reshape(groups, rows, columns)
-
-    def exchange(axis, phase, peers, source, target, place):
-        for d in peers:
-            to = peer(axis, d)
-            pltpu.make_async_remote_copy(
-                src_ref=source(to),
-                dst_ref=target.at[place],
-                send_sem=send_sem.at[phase],
-                recv_sem=recv_sem.at[phase],
-                device_id={axis: to},
-                device_id_type=MESH,
-            ).start()
-        blocks = target.at[: len(peers)]
-        finish.append(pltpu.make_async_copy(blocks, blocks, send_sem.at[phase]).wait)
-        return pltpu.make_async_copy(blocks, blocks, recv_sem.at[phase]).wait
-
-    other_core = {"dp": peer("dp", (0, 0, 1))}
-
-    def gather(phase, block, target):
-        arrive = exchange("dp", phase, DP_PEERS, lambda to: block, target, dp)
-        target[dp] = block[...]
-        return arrive
-
-    arrive = gather(0, values, all_values)
-    loads[1].wait()
-    residual_rows[...] = residual_held[...].astype(jnp.float32).T
-    loads[0].wait()
-    arrive()
-    attended = lax.dot_general(
-        all_values[...].reshape(groups * rows, -1),
-        out_held[...],
-        NT,
-        preferred_element_type=jnp.float32,
-    )
-    in_blocks(out_send, attended)
-
-    arrive = exchange("tp", 2, TP_PEERS, lambda to: out_send.at[to], out_recv, tp)
-    out_recv[tp] = out_send[tp]
-    arrive()
-    own = residual_rows[pl.ds(pl.multiple_of(tp * rows, rows), rows), :]
-    own = own + jnp.sum(out_recv[:, :, :columns].astype(jnp.float32), axis=0)
-    own = own.astype(jnp.bfloat16)
-    stream_rows[tp, :, :columns] = own
-
-    arrive = exchange("tp", 3, TP_PEERS, lambda to: stream_rows.at[tp], stream_rows, tp)
-    loads[2].wait()
-    loads[3].wait()
-    loads[4].wait()
-    arrive()
-    stream = stream_rows[:, :, :columns].astype(jnp.float32).reshape(groups * rows, columns)
-    squares = jnp.sum(stream * stream, axis=1, keepdims=True)
-    scaled = (stream * gain[...].astype(jnp.float32)[None, :]).astype(jnp.bfloat16)
-    high = squares.astype(jnp.bfloat16).astype(jnp.float32)
-    lane = lax.broadcasted_iota(jnp.int32, (groups * rows, 128), 1)
-    split = jnp.where(lane == 0, high, jnp.where(lane == 1, squares - high, 0.0))
-
-    def swap(part, wide, pair_send, pair_recv):
-        chips = groups // 2
-        blocks = wide.astype(jnp.bfloat16).reshape(chips, 2, rows, -1)
-        pair_send[0] = blocks[:, 0]
-        pair_send[1] = blocks[:, 1]
+    def send(block, place, device, phase):
         copy = pltpu.make_async_remote_copy(
-            src_ref=pair_send.at[1 - core],
-            dst_ref=pair_recv,
-            send_sem=send_sem.at[5 + part],
-            recv_sem=recv_sem.at[5 + part],
-            device_id=other_core,
+            src_ref=block,
+            dst_ref=place,
+            send_sem=send_sem.at[phase],
+            recv_sem=recv_sem.at[phase],
+            device_id=device,
             device_id_type=MESH,
         )
         copy.start()
         return copy
 
-    gate = jnp.dot(scaled, gate_held[...], preferred_element_type=jnp.float32)
-    gate_copy = swap(0, gate, gate_pair, gate_other)
-    up = jnp.dot(scaled, up_held[...], preferred_element_type=jnp.float32)
-    up = jnp.concatenate([up, split], axis=1)
-    up_copy = swap(1, up, up_pair, up_other)
-
-    def scatter(part, copy, pair_send, pair_recv, send, recv):
-        copy.wait_recv()
-        finish.append(copy.wait_send)
-        both = pair_send[core].astype(jnp.float32) + pair_recv[...].astype(jnp.float32)
-        send[...] = both.astype(jnp.bfloat16)
-        arrive = exchange(
-            "dp", 7 + part, CHIP_PEERS, lambda to: send.at[to // 2], recv, chip
-        )
-        recv[chip] = send[chip]
+    def exchange(axis, phase, source, target, place):
+        peers = CHIP_PEERS if axis == "dp" else TP_PEERS
+        for d in peers:
+            to = along(axis, d)
+            at = to["dp"] // 2 if axis == "dp" else to["tp"]
+            send(source(at), target.at[place], to, phase)
+        blocks = target.at[: len(peers)]
+        finish.append(pltpu.make_async_copy(blocks, blocks, send_sem.at[phase]).wait)
+        return pltpu.make_async_copy(blocks, blocks, recv_sem.at[phase]).wait
+
+    def gather(phase, block, target):
+        arrive = exchange("dp", phase, lambda to: block, target, chip)
+        target[chip] = block[...]
         return arrive
 
-    gate_arrive = scatter(0, gate_copy, gate_pair, gate_other, gate_send, gate_recv)
-    up_arrive = scatter(1, up_copy, up_pair, up_other, up_send, up_recv)
-    gate_arrive()
-    gate = jnp.sum(gate_recv[...].astype(jnp.float32), axis=0)
-    up_arrive()
-    up = jnp.sum(up_recv[...].astype(jnp.float32), axis=0)
-    squares = up[:, units : units + 1] + up[:, units + 1 : units + 2]
-    inv_rms = 1.0 / jnp.sqrt(squares / model + 1e-06)
-    gate = gate * inv_rms
-    up = up[:, :units] * inv_rms
-    hidden = gate / (1.0 + jnp.exp(-gate)) * up
-    hidden_block[...] = hidden.astype(jnp.bfloat16)
-
-    arrive = gather(1, hidden_block, hidden_rows)
+    def swap(phase, source, held):
+        finish.append(send(source, held.at[core], other_core, phase).wait_send)
+        theirs = held.at[1 - core]
+        return pltpu.make_async_copy(theirs, theirs, recv_sem.at[phase]).wait
+
+    arrive = gather(0, values, all_values)
+    loads[2].wait()
+    own_gain = gain[...].astype(jnp.float32)[None, :]
+    gains[core, :, :columns] = jnp.broadcast_to(own_gain, (rows, columns)).astype(jnp.bfloat16)
+    out_swap = swap(9, w_out, out_held)
+    residual_swap = swap(10, residual, residual_held)
+    gain_swap = swap(11, gains.at[core], gains)
+    gate_swap = swap(12, w_gate, gate_held)
+    up_swap = swap(13, w_up, up_held)
+    down_swap = swap(14, w_down, down_held)
+    loads[1].wait()
+    residual_swap()
+    for side in range(2):
+        residual_rows[side] = residual_held[side].astype(jnp.float32).T
+    loads[0].wait()
+    out_swap()
+    arrive()
+    every = all_values[...].reshape(chips * rows, -1)
+    for side in range(2):
+        attended = lax.dot_general(every, out_held[side], NT, preferred_element_type=jnp.float32)
+        attended = attended.astype(jnp.bfloat16).reshape(chips, rows, columns)
+        out_send[:, side, :, :columns] = attended
+
+    arrive = exchange("tp", 3, lambda to: out_send.at[to // 2, lax.rem(to, 2)], out_recv, tp)
+    out_recv[tp] = out_send[z, x_lo]
+    arrive()
+    own_rows = pl.ds(pl.multiple_of((2 * z + core) * rows, rows), rows)
+    own = residual_rows[x_lo, own_rows, :]
+    own = own + jnp.sum(out_recv[:, :, :columns].astype(jnp.float32), axis=0)
+    own = own.astype(jnp.bfloat16).astype(jnp.float32)
+    squares = jnp.sum(own * own, axis=1, keepdims=True)
+    high = squares.astype(jnp.bfloat16).astype(jnp.float32)
+    lane = lax.broadcasted_iota(jnp.int32, (rows, stream_own.shape[1] - columns), 1)
+    split = jnp.where(lane == 0, high, jnp.where(lane == 1, squares - high, 0.0))
+    stream_own[...] = jnp.concatenate([own, split], axis=1).astype(jnp.bfloat16)
+
+    arrive = exchange("tp", 4, lambda to: stream_own, stream_rows, tp)
+    stream_rows[tp] = stream_own[...]
+    for load in loads[3:5]:
+        load.wait()
+    gain_swap()
+    gate_swap()
+    up_swap()
+    arrive()
+    finish.append(send(stream_rows.at[2 * z + 1 - core], base, other_core, 6).wait_send)
+    base_arrive = pltpu.make_async_copy(base, base, recv_sem.at[6]).wait
+    scaled, tail = [], 0.0
+    for side in range(2):
+        part = jnp.stack([stream_rows[2 * k + side] for k in range(chips)])
+        part = part.astype(jnp.float32)
+        tail += part[:, :, columns // 128 * 128 :]
+        part = part[:, :, :columns].reshape(chips * rows, columns)
+        scaled.append((part * gains[side, :1, :columns].astype(jnp.float32)).astype(jnp.bfloat16))
+
+    first = hidden_block.shape[1]
+    parts = [
+        (slice(0, first), (first_send, first_recv)),
+        (slice(first, units), (second_send, second_recv)),
+    ]
+    arrivals = []
+    for part, (some, (block, recv)) in enumerate(parts):
+        at = 0
+        for held_weight in (gate_held, up_held):
+            product = sum(
+                jnp.dot(
+                    scaled[side], held_weight[side, :, some], preferred_element_type=jnp.float32
+                )
+                for side in range(2)
+            )
+            product = product.astype(jnp.bfloat16).reshape(chips, rows, -1)
+            block[:, :, at : at + product.shape[2]] = product
+            at += product.shape[2]
+        if part == 0:
+            block[:, :, at:] = tail.astype(jnp.bfloat16)
+        arrivals.append(exchange("dp", 7 + part, lambda to: block.at[to], recv, chip))
+        recv[chip] = block[chip]
+    gathers = []
+    for part, (arrive, (some, refs)) in enumerate(zip(arrivals, parts)):
+        width = some.stop - some.start
+        arrive()
+        sums = jnp.sum(refs[1][...].astype(jnp.float32), axis=0)
+        if part == 0:
+            at = 2 * width + columns % 128
+            squares = sums[:, at : at + 1] + sums[:, at + 1 : at + 2]
+            inv_rms = 1.0 / jnp.sqrt(squares / model + 1e-06)
+        gate = sums[:, :width] * inv_rms
+        up = sums[:, width : 2 * width] * inv_rms
+        hidden = gate / (1.0 + jnp.exp(-gate)) * up
+        block, target = ((hidden_block, hidden_rows), (rest_block, rest_rows))[part]
+        block[...] = hidden.astype(jnp.bfloat16)
+        gathers.append(gather(1 + part, block, target))
+
     loads[5].wait()
-    arrive()
-    down = lax.dot_general(
-        hidden_rows[...].reshape(groups * rows, units),
-        down_held[...],
-        NT,
-        preferred_element_type=jnp.float32,
-    )
-    in_blocks(down_send, down)
-
-    arrive = exchange("tp", 4, TP_PEERS, lambda to: down_send.at[to], down_recv, tp)
-    down_recv[tp] = down_send[tp]
-    arrive()
+    down_swap()
+    down = [0.0, 0.0]
+    sides = (1 - core, core)
+    for arrive, target, (some, _) in zip(gathers, (hidden_rows, rest_rows), parts):
+        arrive()
+        hidden = target[...].reshape(chips * rows, -1)
+        for at, side in enumerate(sides):
+            down[at] += lax.dot_general(
+                hidden, down_held[side, :, some], NT, preferred_element_type=jnp.float32
+            )
+
+    def down_blocks(at):
+        product = down[at].astype(jnp.bfloat16).reshape(chips, rows, columns)
+        down_send[sides[at], :, :, :columns] = product
+
+    def scatter(blocks, half):
+        for dz in sorted(range(8), key=lambda d: -min(d, 8 - d)):
+            k = lax.rem(z + dz, 8)
+            to = 2 * k + half
+
+            def give(k=k, to=to):
+                send(blocks.at[k], down_recv.at[tp], {"tp": to}, 5)
+
+            if dz:
+                give()
+            else:
+                pl.when(to != tp)(give)
+
+                @pl.when(to == tp)
+                def _():
+                    down_recv[tp] = blocks[z]
+
+    down_blocks(0)
+    finish.append(send(down_send.at[1 - core], down_other, other_core, 15).wait_send)
+    down_blocks(1)
+    scatter(down_send.at[core], core)
+    pltpu.make_async_copy(down_other, down_other, recv_sem.at[15]).wait()
+    scatter(down_other, 1 - core)
+    blocks = down_recv.at[: groups - 1]
+    finish.append(pltpu.make_async_copy(blocks, blocks, send_sem.at[5]).wait)
+    pltpu.make_async_copy(blocks, blocks, recv_sem.at[5]).wait()
+    base_arrive()
+    stream = jnp.where(core == x_lo, stream_rows[2 * z + core], base[...])[:, :columns]
     result = jnp.sum(down_recv[:, :, :columns].astype(jnp.float32), axis=0)
-    mixed[...] = (own.astype(jnp.float32) + result).astype(jnp.bfloat16)
+    mixed[...] = (stream.astype(jnp.float32) + result).astype(jnp.bfloat16)
     for sent in finish:
         sent()
 
@@ -425,11 +475,14 @@
     rows, heads, depth = queries.shape
     columns, units = w_down.shape
     wide = -(-columns // 128) * 128
+    rest = units // 256 * 128
+    first = units - rest
     vmem = pl.BlockSpec(memory_space=pltpu.VMEM)
     anywhere = pl.BlockSpec(memory_space=pl.ANY)
     blocks = lambda width: pltpu.VMEM((groups, rows, width), jnp.bfloat16)
     half = lambda width: pltpu.VMEM((groups // 2, rows, width), jnp.bfloat16)
-    pair = lambda width: pltpu.VMEM((2, groups // 2, rows, width), jnp.bfloat16)
+    sides = lambda width: pltpu.VMEM((groups // 2, 2, rows, width), jnp.bfloat16)
+    both = lambda array: pltpu.VMEM((2, *array.shape), jnp.bfloat16)
     return pl.pallas_call(
         functools.partial(layer_kernel, model),
         out_shape=jax.ShapeDtypeStruct((rows, columns), jnp.bfloat16),
@@ -444,34 +497,36 @@
             pltpu.VMEM(stats.shape, jnp.float32),
             pltpu.VMEM((heads, rows, KVR), jnp.float32),
             pltpu.VMEM((rows, heads * VD), jnp.bfloat16),
-            pltpu.VMEM(w_out.shape, jnp.bfloat16),
-            pltpu.VMEM(w_gate.shape, jnp.bfloat16),
-            pltpu.VMEM(w_up.shape, jnp.bfloat16),
-            pltpu.VMEM(w_down.shape, jnp.bfloat16),
-            pltpu.VMEM(residual.shape, jnp.bfloat16),
+            both(w_out),
+            both(w_gate),
+            both(w_up),
+            both(w_down),
+            both(residual),
             pltpu.VMEM(gain.shape, jnp.bfloat16),
-            pltpu.VMEM(residual.shape[::-1], jnp.float32),
-            blocks(heads * VD),
+            pltpu.VMEM((2, *residual.shape[::-1]), jnp.float32),
+            half(heads * VD),
+            sides(wide),
             blocks(wide),
+            pltpu.VMEM((2, rows, wide), jnp.bfloat16),
+            pltpu.VMEM((rows, wide), jnp.bfloat16),
             blocks(wide),
-            blocks(wide),
-            pair(units),
-            half(units),
-            half(units),
-            half(units),
-            pair(units + 128),
-            half(units + 128),
-            half(units + 128),
-            half(units + 128),
-            pltpu.VMEM((rows, units), jnp.bfloat16),
-            blocks(units),
-            blocks(wide),
+            pltpu.VMEM((rows, wide), jnp.bfloat16),
+            half(2 * first + 128),
+            half(2 * first + 128),
+            half(2 * rest),
+            half(2 * rest),
+            pltpu.VMEM((rows, first), jnp.bfloat16),
+            half(first),
+            pltpu.VMEM((rows, rest), jnp.bfloat16),
+            half(rest),
+            pltpu.VMEM((2, groups // 2, rows, wide), jnp.bfloat16),
+            half(wide),
             blocks(wide),
             pltpu.SemaphoreType.DMA((5,)),
             pltpu.SemaphoreType.DMA((rows,)),
             pltpu.SemaphoreType.DMA((6,)),
-            pltpu.SemaphoreType.DMA((9,)),
-            pltpu.SemaphoreType.DMA((9,)),
+            pltpu.SemaphoreType.DMA((16,)),
+            pltpu.SemaphoreType.DMA((16,)),
         ],
         compiler_params=pltpu.CompilerParams(
             collective_id=0, has_side_effects=True, vmem_limit_bytes=VMEM_BYTES

time: 54.8 us -> 53.2 us (0.971)
  Pallas kernels: 53.3 us -> 51.7 us
    pallas_call x1, Pallas kernels: 3.96 us -> 2.34 us  [attend_later(): pl.pallas_call(later_kernel, out_shape=[jax.ShapeDtypeStruct((requests, h...]
where the time goes in v6:
time: 53.2 us; the launch traced here: 53 us
  Pallas kernels  51.7 us (97%)
  local copies, waits for them, and re-layouts  1.3 us (2%)
    pallas_call x1, Pallas kernels, layer(): pl.pallas_call(functools.partial(layer_kernel, model), out_shape=jax.Shap...  49.4 us
    pallas_call x1, Pallas kernels, attend_later(): pl.pallas_call(later_kernel, out_shape=[jax.ShapeDtypeStruct((requests, h...  2.34 us
    unnamed x1, local copies, waits for them, and re-layouts  1.3 us

profile of v6, /device:TPU:1, one launch (start us, length us, event | category | flops | bytes accessed | tf_op | source)
XLA Modules:
  0.0 53.0 jit_solution(9794770915255657509)
XLA Ops:
  0.0 2.3 %attend_later.1 = (bf16[8,8,576]{2,1,0:T(8,128)(2,1)}, f32[8,8,512]{2,1,0:T(8,128)}, f32[2,8,8,128]{3,2,1,0:T(8,128)}) custom-call(s32[8]{0:T(128)} %lengths_in.3, bf16[8,1536]{1,0:T(8,128)(2,1)} %query_in.1, bf16[8,576,2048]{2,1,0:T(8,128)(2,1)} %bitcast.4, bf16[8,128,512]{2,1,0:T(8,128)(2,1)} %w_uk.1), custom_call_target="tpu_custom_call" | custom-call | tf_op jit(solution)/shard_map/attend_later/pallas_call | solution.py:121
  2.3 49.4 %layer.1 = bf16[8,448]{1,0:T(8,128)(2,1)} custom-call(s32[8]{0:T(128)} %lengths_in.3, bf16[8,576,2048]{2,1,0:T(8,128)(2,1)} %bitcast.5, bf16[8,512,128]{2,1,0:T(8,128)(2,1)} %w_value.1, bf16[8,8,576]{2,1,0:T(8,128)(2,1)} %get-tuple-element.8.queries_in, f32[8,8,512]{2,1,0:T(8,128)} %get-tuple-element.9.sums_in, f32[2,8,8,128]{3,2,1,0:T(8,128)} %get-tuple-element.10.stats_in, ...), custom_call_target="tpu_custom_call" | custom-call | tf_op jit(solution)/shard_map/layer/pallas_call | solution.py:486
  51.7 1.3 %copy.13 = bf16[8,448]{1,0:T(8,128)(2,1)} copy(bf16[8,448]{1,0:T(8,128)(2,1)} %layer.1) | data formatting | bytes 14336

commit v7 on v6

--- a/solution.py
+++ b/solution.py
@@ -81,8 +81,11 @@
         @pl.loop(0, requests)
         def _(b):
             chunks = lax.div(lengths[b] - 1, FIRST)
-            for k in range(1, most + 1):
-                pl.when(chunks == k)(lambda k=k: step(b, k * FIRST))
+
+            @pl.when(chunks > 0)
+            def _():
+                for k in range(1, most + 1):
+                    pl.when(chunks == k)(lambda k=k: step(b, k * FIRST))
 
     def copy(b, width):
         return pltpu.make_async_copy(
@@ -168,6 +171,8 @@
     gate_held,
     up_held,
     down_held,
+    out_turned,
+    down_turned,
     residual_held,
     gain,
     residual_rows,
@@ -187,7 +192,6 @@
     rest_block,
     rest_rows,
     down_send,
-    down_other,
     down_recv,
     attend_sem,
     cache_sem,
@@ -247,7 +251,7 @@
     other_core = {"dp": other_dp, "tp": tp}
     barrier = pltpu.get_barrier_semaphore()
     partners = [along("dp", d) for d in CHIP_PEERS] + [along("tp", d) for d in TP_PEERS]
-    partners.append(other_core)
+    partners += [{"dp": other_dp, **along("tp", d)} for d in TP_PEERS] + [other_core]
     for partner in partners:
         pl.semaphore_signal(barrier, inc=1, device_id=partner, device_id_type=MESH)
 
@@ -329,11 +333,13 @@
     for side in range(2):
         residual_rows[side] = residual_held[side].astype(jnp.float32).T
     loads[0].wait()
+    out_turned[core] = out_held[core].T
     out_swap()
+    out_turned[1 - core] = out_held[1 - core].T
     arrive()
     every = all_values[...].reshape(chips * rows, -1)
     for side in range(2):
-        attended = lax.dot_general(every, out_held[side], NT, preferred_element_type=jnp.float32)
+        attended = jnp.dot(every, out_turned[side], preferred_element_type=jnp.float32)
         attended = attended.astype(jnp.bfloat16).reshape(chips, rows, columns)
         out_send[:, side, :, :columns] = attended
 
@@ -390,6 +396,10 @@
             block[:, :, at:] = tail.astype(jnp.bfloat16)
         arrivals.append(exchange("dp", 7 + part, lambda to: block.at[to], recv, chip))
         recv[chip] = block[chip]
+    loads[5].wait()
+    down_swap()
+    for side in range(2):
+        down_turned[side] = down_held[side].T
     gathers = []
     for part, (arrive, (some, refs)) in enumerate(zip(arrivals, parts)):
         width = some.stop - some.start
@@ -406,52 +416,55 @@
         block[...] = hidden.astype(jnp.bfloat16)
         gathers.append(gather(1 + part, block, target))
 
-    loads[5].wait()
-    down_swap()
     down = [0.0, 0.0]
-    sides = (1 - core, core)
     for arrive, target, (some, _) in zip(gathers, (hidden_rows, rest_rows), parts):
         arrive()
         hidden = target[...].reshape(chips * rows, -1)
-        for at, side in enumerate(sides):
-            down[at] += lax.dot_general(
-                hidden, down_held[side, :, some], NT, preferred_element_type=jnp.float32
+        for side in range(2):
+            down[side] += jnp.dot(
+                hidden, down_turned[side, some, :], preferred_element_type=jnp.float32
             )
-
-    def down_blocks(at):
-        product = down[at].astype(jnp.bfloat16).reshape(chips, rows, columns)
-        down_send[sides[at], :, :, :columns] = product
-
-    def scatter(blocks, half):
-        for dz in sorted(range(8), key=lambda d: -min(d, 8 - d)):
-            k = lax.rem(z + dz, 8)
-            to = 2 * k + half
-
-            def give(k=k, to=to):
-                send(blocks.at[k], down_recv.at[tp], {"tp": to}, 5)
-
-            if dz:
-                give()
+    for side in range(2):
+        product = down[side].astype(jnp.bfloat16).reshape(chips, rows, columns)
+        down_send[:, side, :, :columns] = product
+
+    kept = core == x_lo
+    for dz in sorted(range(8), key=lambda d: -min(d, 8 - d)):
+        k = lax.rem(z + dz, 8)
+        for side in (1 - core, core):
+            device = {"dp": chip * 2 + side, "tp": 2 * k + core}
+
+            def give(phase, k=k, side=side, device=device):
+                send(down_send.at[k, side], down_recv.at[tp], device, phase)
+
+            if dz == 0 and side is core:
+                pl.when(jnp.logical_not(kept))(lambda give=give: give(15))
             else:
-                pl.when(to != tp)(give)
-
-                @pl.when(to == tp)
-                def _():
-                    down_recv[tp] = blocks[z]
-
-    down_blocks(0)
-    finish.append(send(down_send.at[1 - core], down_other, other_core, 15).wait_send)
-    down_blocks(1)
-    scatter(down_send.at[core], core)
-    pltpu.make_async_copy(down_other, down_other, recv_sem.at[15]).wait()
-    scatter(down_other, 1 - core)
-    blocks = down_recv.at[: groups - 1]
-    finish.append(pltpu.make_async_copy(blocks, blocks, send_sem.at[5]).wait)
-    pltpu.make_async_copy(blocks, blocks, recv_sem.at[5]).wait()
+                give(5)
+
+    @pl.when(kept)
+    def _():
+        down_recv[tp] = down_send[z, core]
+
+    def wait_down(sem, blocks):
+        blocks = down_recv.at[:blocks]
+        pltpu.make_async_copy(blocks, blocks, sem).wait()
+
+    @pl.when(kept)
+    def _():
+        wait_down(recv_sem.at[5], groups - 2)
+        wait_down(recv_sem.at[15], 1)
+
+    @pl.when(jnp.logical_not(kept))
+    def _():
+        wait_down(recv_sem.at[5], groups)
+
     base_arrive()
-    stream = jnp.where(core == x_lo, stream_rows[2 * z + core], base[...])[:, :columns]
+    stream = jnp.where(kept, stream_rows[2 * z + core], base[...])[:, :columns]
     result = jnp.sum(down_recv[:, :, :columns].astype(jnp.float32), axis=0)
     mixed[...] = (stream.astype(jnp.float32) + result).astype(jnp.bfloat16)
+    wait_down(send_sem.at[5], groups - 1)
+    pl.when(jnp.logical_not(kept))(lambda: wait_down(send_sem.at[15], 1))
     for sent in finish:
         sent()
 
@@ -501,6 +514,8 @@
             both(w_gate),
             both(w_up),
             both(w_down),
+            pltpu.VMEM((2, *w_out.shape[::-1]), jnp.bfloat16),
+            pltpu.VMEM((2, *w_down.shape[::-1]), jnp.bfloat16),
             both(residual),
             pltpu.VMEM(gain.shape, jnp.bfloat16),
             pltpu.VMEM((2, *residual.shape[::-1]), jnp.float32),
@@ -519,8 +534,7 @@
             half(first),
             pltpu.VMEM((rows, rest), jnp.bfloat16),
             half(rest),
-            pltpu.VMEM((2, groups // 2, rows, wide), jnp.bfloat16),
-            half(wide),
+            sides(wide),
             blocks(wide),
             pltpu.SemaphoreType.DMA((5,)),
             pltpu.SemaphoreType.DMA((rows,)),

time: 53.2 us -> 52.4 us (0.985)
  Pallas kernels: 51.7 us -> 50.9 us
    pallas_call x1, Pallas kernels: 49.4 us -> 48.6 us  [layer(): pl.pallas_call(functools.partial(layer_kernel, model), out_shape=jax.Shap...]
where the time goes in v7:
time: 52.4 us; the launch traced here: 52.3 us
  Pallas kernels  50.9 us (97%)
  local copies, waits for them, and re-layouts  1.3 us (2%)
    pallas_call x1, Pallas kernels, layer(): pl.pallas_call(functools.partial(layer_kernel, model), out_shape=jax.Shap...  48.6 us
    pallas_call x1, Pallas kernels, attend_later(): pl.pallas_call(later_kernel, out_shape=[jax.ShapeDtypeStruct((requests, h...  2.34 us
    unnamed x1, local copies, waits for them, and re-layouts  1.3 us

profile of v7, /device:TPU:1, one launch (start us, length us, event | category | flops | bytes accessed | tf_op | source)
XLA Modules:
  0.0 52.3 jit_solution(2153527754011916316)
XLA Ops:
  0.0 2.3 %attend_later.1 = (bf16[8,8,576]{2,1,0:T(8,128)(2,1)}, f32[8,8,512]{2,1,0:T(8,128)}, f32[2,8,8,128]{3,2,1,0:T(8,128)}) custom-call(s32[8]{0:T(128)} %lengths_in.3, bf16[8,1536]{1,0:T(8,128)(2,1)} %query_in.1, bf16[8,576,2048]{2,1,0:T(8,128)(2,1)} %bitcast.4, bf16[8,128,512]{2,1,0:T(8,128)(2,1)} %w_uk.1), custom_call_target="tpu_custom_call" | custom-call | tf_op jit(solution)/shard_map/attend_later/pallas_call | solution.py:124
  2.3 48.6 %layer.1 = bf16[8,448]{1,0:T(8,128)(2,1)} custom-call(s32[8]{0:T(128)} %lengths_in.3, bf16[8,576,2048]{2,1,0:T(8,128)(2,1)} %bitcast.5, bf16[8,512,128]{2,1,0:T(8,128)(2,1)} %w_value.1, bf16[8,8,576]{2,1,0:T(8,128)(2,1)} %get-tuple-element.8.queries_in, f32[8,8,512]{2,1,0:T(8,128)} %get-tuple-element.9.sums_in, f32[2,8,8,128]{3,2,1,0:T(8,128)} %get-tuple-element.10.stats_in, ...), custom_call_target="tpu_custom_call" | custom-call | tf_op jit(solution)/shard_map/layer/pallas_call | solution.py:499
  51.0 1.3 %copy.13 = bf16[8,448]{1,0:T(8,128)(2,1)} copy(bf16[8,448]{1,0:T(8,128)(2,1)} %layer.1) | data formatting | bytes 14336
